TPU v7x, 256 devices: a whole 4x4x8 slice. The times are simulated.
256 devices in a mesh: rep: 32 (over z, y), rack: 8 (over x, core).
Axes of the slice: x: 4, y: 4, z: 8, core: 2. Of those that a mesh axis runs over, the one named last changes fastest.
Arguments:
- grads: bfloat16 [64, 1024, 1024], P('rep', 'rack'), may hold values from -3 to 3
- left: bfloat16 [64, 1024, 1024], P('rep', 'rack'), may hold values from -1 to 3, as said below
- right: bfloat16 [64, 1024, 1024], P('rep', 'rack'), may hold values from -1 to 3, as said below
- left_root: bfloat16 [64, 1024, 1024], P('rep', 'rack'), may hold values from -1 to 3, as said below
- right_root: bfloat16 [64, 1024, 1024], P('rep', 'rack'), may hold values from -1 to 3, as said below
- second: bfloat16 [64, 1024, 1024], P('rep', 'rack'), may hold values from 9.9658966e-05 to 0.0099487305
- owner: int32 [32], replicated, may hold values from 0 to 31, as said below
Outputs:
- left_new: bfloat16 [64, 1024, 1024], P('rep', 'rack')
- right_new: bfloat16 [64, 1024, 1024], P('rep', 'rack')
- second_new: bfloat16 [64, 1024, 1024], P('rep', 'rack')
- directions: bfloat16 [32, 1024, 1024], P(None, 'rack')
Inputs may be any that keep to these rules, and one draw needn't show every extreme that they name: Each owner holds at most 2 blocks and some owner holds exactly 2. `left`: symmetric in the last two dimensions. `right`: symmetric in the last two dimensions. `left_root`: symmetric in the last two dimensions. `right_root`: symmetric in the last two dimensions.
All inputs are finite; a program needn't handle non-finite values.
Results may differ from a plain program's by a relative error of at most 0.017.
Values may be sent and summed in bfloat16 or wider, within the bound.
A program may use at most 128 MiB of HBM per device.

v0:
```python
import jax
import jax.numpy as jnp
from jax import lax
from jax.sharding import PartitionSpec as P


def block_places(owner, slots_dev):
    count = owner.shape[0]
    spots = jnp.arange(count, dtype=jnp.int32)
    earlier = (owner[None, :] == owner[:, None]) & (spots[None, :] < spots[:, None])
    slot = jnp.sum(earlier.astype(jnp.int32), axis=1)
    return owner * slots_dev + slot


def on_device(grads, left, right, left_root, right_root, second, owner):
    replica = lax.axis_index("rep")
    slots_dev, rows, width = grads.shape
    place = block_places(owner, slots_dev)
    held = jnp.sum((owner == replica).astype(jnp.int32))
    used = jnp.arange(slots_dev, dtype=jnp.int32) < held
    piece = lax.all_gather(grads, "rack", axis=1, tiled=True)
    outer = jnp.einsum("srk,snk->srn", grads, piece, preferred_element_type=jnp.float32)
    mixed_acc = jnp.einsum("srn,snk->srk", left_root, piece, preferred_element_type=jnp.float32)
    inner_rows = jnp.transpose(
        lax.psum_scatter(
            jnp.einsum("sjr,sjk->rsk", grads, grads, preferred_element_type=jnp.float32).astype(
                jnp.bfloat16
            ),
            "rack",
            scatter_dimension=0,
            tiled=True,
        ).astype(jnp.float32),
        (1, 0, 2),
    )
    keep = used[:, None, None]
    left_new = jnp.where(
        keep, (0.95 * left.astype(jnp.float32) + 0.05 * outer).astype(jnp.bfloat16), left
    )
    right_new = jnp.where(
        keep, (0.95 * right.astype(jnp.float32) + 0.05 * inner_rows).astype(jnp.bfloat16), right
    )
    mixed_b = mixed_acc.astype(jnp.bfloat16)
    prec = jnp.einsum(
        "srn,snk->srk",
        mixed_b,
        lax.all_gather(right_root, "rack", axis=1, tiled=True),
        preferred_element_type=jnp.float32,
    )
    prec_b = lax.optimization_barrier(prec.astype(jnp.bfloat16))
    grad32 = grads.astype(jnp.float32)
    moment = 0.95 * second.astype(jnp.float32) + 0.05 * grad32 * grad32
    second_new = jnp.where(keep, moment.astype(jnp.bfloat16), second)
    adam = grad32 / (jnp.sqrt(moment) + 1e-08)
    partial_sums = jnp.stack(
        [jnp.sum(adam * adam, axis=(1, 2)), jnp.sum(prec * prec, axis=(1, 2))], axis=1
    )
    totals = lax.psum(partial_sums, "rack")
    scale = jnp.sqrt(totals[:, 0]) / jnp.sqrt(totals[:, 1] + 1e-06)
    scaled = (prec_b.astype(jnp.float32) * scale[:, None, None]).astype(jnp.bfloat16)
    gathered = lax.all_gather(scaled, "rep", axis=0, tiled=True)
    directions = jnp.take(gathered, place, axis=0)
    return (left_new, right_new, second_new, directions)


def solution(mesh):
    in_specs = (
        P("rep", "rack", None),
        P("rep", "rack", None),
        P("rep", "rack", None),
        P("rep", "rack", None),
        P("rep", "rack", None),
        P("rep", "rack", None),
        P(),
    )
    out_specs = (
        P("rep", "rack", None),
        P("rep", "rack", None),
        P("rep", "rack", None),
        P(None, "rack", None),
    )
    return jax.shard_map(
        on_device, mesh=mesh, in_specs=in_specs, out_specs=out_specs, check_vma=False
    )
```

profile of v0, /device:TPU:1, one launch (start us, length us, event | category | flops | bytes accessed | tf_op | source)
XLA Modules:
  0.0 295.3 jit_solution(9203472068554112803)
XLA Ops:
  7.2 0.0 all-gather.6.cloned.1.call-start
  7.2 0.7 all-gather.6.cloned.1.call-update
  7.9 0.0 all-gather.4.cloned.1.call-start
  8.0 0.7 all-gather.4.cloned.1.call-update
  8.7 0.0 reduce-scatter.2.cloned.1.call-start
  8.7 4.6 %convert_bitcast_fusion = bf16[1024,2,1024]{2,0,1:T(8,128)(2,1)} fusion(bf16[2,128,1024]{2,1,0:T(8,128)(2,1)} %param.7), kind=kOutput, calls=%fused_computation.2 | convolution fusion | flops 538968064 | bytes 4718592 | tf_op jit(solution)/shard_map/sjr,sjk->rsk/dot_general | solution.py:26
  13.3 0.0 reduce-scatter.2.cloned.1.call-update
  13.3 0.0 all-gather.8.cloned.1.call-start
  13.4 0.7 fusion.8
  14.1 34.6 %all-gather.6.cloned.1.call-done = bf16[2,1024,1024]{2,1,0:T(8,128)(2,1)} async-done(((bf16[2,128,1024]{2,1,0:T(8,128)(2,1)}), bf16[2,1024,1024]{2,1,0:T(8,128)(2,1)}) %all-gather.6.cloned.1.call-update) | async-done | bytes 4194320 | tf_op jit(solution)/shard_map/all_gather | solution.py:46
  48.7 36.5 %all-gather.4.cloned.1.call-done = bf16[2,1024,1024]{2,1,0:T(8,128)(2,1)} async-done(((bf16[2,128,1024]{2,1,0:T(8,128)(2,1)}), bf16[2,1024,1024]{2,1,0:T(8,128)(2,1)}) %all-gather.4.cloned.1.call-update) | async-done | bytes 4194320 | tf_op jit(solution)/shard_map/all_gather | solution.py:21
  85.3 4.9 %multiply_reduce_fusion = (f32[2]{0:T(128)S(1)}, bf16[2,128,1024]{2,1,0:T(8,128)(2,1)S(1)}) fusion(bf16[2,1024,1024]{2,1,0:T(8,128)(2,1)} %all-gather.6.cloned.1.call-done, bf16[2,128,1024]{2,1,0:T(8,128)(2,1)S(1)} %copy-done, bf16[2,1024,1024]{2,1,0:T(8,128)(2,1)} %all-gather.4.cloned.1.call-done), kind=kOutput, calls=%fused_computation.16 | convolution fusion | flops 1074790400 | bytes 9437192 | tf_op jit(solution)/shard_map/srn,snk->srk/dot_general | solution.py:43
  90.1 12.2 %psum.7 = f32[2,2]{0,1:T(2,128)S(1)} all-reduce(f32[2,2]{0,1:T(2,128)S(1)} %pad_maximum_fusion), channel_id=1, replica_groups=mesh['rep'=32,'rack'=8] {'rack'}, use_global_device_ids=true, to_apply=%region_5.6 | all-reduce | flops 4 | bytes 32 | tf_op jit(solution)/shard_map/psum | solution.py:57
  102.3 1.0 multiply_convert_fusion
  103.3 0.0 all-gather.8.cloned.1.call-update
  103.3 0.6 fusion.12
  104.0 0.7 iota_compare_fusion.1
  104.6 0.2 convert_reduce_fusion
  104.8 4.7 %fusion.2 = bf16[2,128,1024]{2,1,0:T(8,128)(2,1)} fusion(bf16[2,128,1024]{2,1,0:T(8,128)(2,1)S(1)} %copy-done.3, bf16[2,128,1024]{2,1,0:T(8,128)(2,1)S(1)} %copy-done.1, bf16[2,1024,1024]{2,1,0:T(8,128)(2,1)} %all-gather.4.cloned.1.call-done, pred[2]{0:T(512)(128)(4,1)S(1)} %iota_compare_fusion.1), kind=kOutput, calls=%fused_computation.9 | convolution fusion | flops 538443776 | bytes 5767170 | tf_op jit(solution)/shard_map/srk,snk->srn/dot_general | solution.py:22
  109.5 16.0 %reduce-scatter.2.cloned.1.call-done = bf16[128,2,1024]{2,0,1:T(8,128)(2,1)} async-done(((bf16[1024,2,1024]{2,0,1:T(8,128)(2,1)}), bf16[128,2,1024]{2,0,1:T(8,128)(2,1)}) %reduce-scatter.2.cloned.1.call-update) | async-done | bytes 524304 | tf_op jit(solution)/shard_map/reduce_scatter | solution.py:25
  125.5 2.6 fusion.9
  128.1 142.1 %all-gather.8.cloned.1.call-done = bf16[64,128,1024]{2,1,0:T(8,128)(2,1)} async-done(((bf16[2,128,1024]{2,1,0:T(8,128)(2,1)}), bf16[64,128,1024]{2,1,0:T(8,128)(2,1)}) %all-gather.8.cloned.1.call-update) | async-done | bytes 16777232 | tf_op jit(solution)/shard_map/all_gather | solution.py:60
  270.2 11.0 %gather_fusion = bf16[32,128,1024]{2,1,0:T(8,128)(2,1)} fusion(bf16[64,128,1024]{2,1,0:T(8,128)(2,1)} %all-gather.8.cloned.1.call-done, s32[1024]{0:T(1024)S(1)} %pad_clamp_fusion), kind=kCustom, calls=%fused_computation | custom fusion | bytes 16777344 | tf_op jit(solution)/shard_map/jit(_take)/gather | solution.py:61
  281.2 7.6 %broadcast_select_fusion = bf16[32,128,1024]{2,1,0:T(8,128)(2,1)} fusion(bf16[32,128,1024]{2,1,0:T(8,128)(2,1)} %gather_fusion, pred[32]{0:T(512)(128)(4,1)S(1)} %get-tuple-element.4), kind=kLoop, calls=%fused_computation.1 | loop fusion | flops 4194304 | bytes 16777248 | tf_op jit(solution)/shard_map/jit(_take)/select_n | solution.py:61
  (16 shorter events, 0.1 us)
Async XLA Ops:
  7.2 78.1 %copy-start = (bf16[2,128,1024]{2,1,0:T(8,128)(2,1)S(1)}, bf16[2,128,1024]{2,1,0:T(8,128)(2,1)}, u32[]{:S(2)}) copy-start(bf16[2,128,1024]{2,1,0:T(8,128)(2,1)} %param.10) | copy-start | bytes 1572868
  7.2 41.6 %all-gather.6.cloned.1.call-start = ((), (), s32[]{:S(2)}) async-start(), calls=%async_computation.3 | async-start | bytes 4718592 | tf_op jit(solution)/shard_map/all_gather | solution.py:46
  7.9 77.3 %all-gather.4.cloned.1.call-start = ((), (), s32[]{:S(2)}) async-start(), calls=%async_computation.1 | async-start | bytes 4718592 | tf_op jit(solution)/shard_map/all_gather | solution.py:21
  8.7 4.7 %copy-start.1 = (bf16[2,128,1024]{2,1,0:T(8,128)(2,1)S(1)}, bf16[2,128,1024]{2,1,0:T(8,128)(2,1)}, u32[]{:S(2)}) copy-start(bf16[2,128,1024]{2,1,0:T(8,128)(2,1)} %param.7) | copy-start | bytes 1572868
  8.7 4.7 %copy-start.2 = (bf16[2,128,1024]{2,1,0:T(8,128)(2,1)S(1)}, bf16[2,128,1024]{2,1,0:T(8,128)(2,1)}, u32[]{:S(2)}) copy-start(bf16[2,128,1024]{2,1,0:T(8,128)(2,1)} %param.12) | copy-start | bytes 1572868
  8.7 116.8 %reduce-scatter.2.cloned.1.call-start = ((), (), s32[]{:S(2)}) async-start(), calls=%async_computation.2 | async-start | bytes 4718592 | tf_op jit(solution)/shard_map/reduce_scatter | solution.py:25
  13.3 256.9 %all-gather.8.cloned.1.call-start = ((), (), s32[]{:S(2)}) async-start(), calls=%async_computation.4 | async-start | bytes 17301504 | tf_op jit(solution)/shard_map/all_gather | solution.py:60
  14.1 89.2 %copy-start.5 = (s32[32]{0:T(128)S(1)}, s32[32]{0:T(128)}, u32[]{:S(2)}) copy-start(s32[32]{0:T(128)} %param.13) | copy-start | bytes 388
  14.1 90.7 %copy-start.3 = (bf16[2,128,1024]{2,1,0:T(8,128)(2,1)S(1)}, bf16[2,128,1024]{2,1,0:T(8,128)(2,1)}, u32[]{:S(2)}) copy-start(bf16[2,128,1024]{2,1,0:T(8,128)(2,1)} %param.8) | copy-start | bytes 1572868
  90.1 35.4 %copy-start.4 = (bf16[2,128,1024]{2,1,0:T(8,128)(2,1)S(1)}, bf16[2,128,1024]{2,1,0:T(8,128)(2,1)}, u32[]{:S(2)}) copy-start(bf16[2,128,1024]{2,1,0:T(8,128)(2,1)} %param.9) | copy-start | bytes 1572868
Sparse Core Ops, SparseCore 0:
  9.9 38.8 all-gather.5
  50.6 34.6 all-gather.3
  88.4 37.0 reduce-scatter.1
  128.0 142.2 all-gather.7
where the time goes:
time: 296 us; the launch traced here: 295 us
  waiting for transfers between devices  231 us (78%)
  matrix products  14.1 us (5%)
  between operations  13.9 us (5%)
  other arithmetic  13.4 us (5%)
  blocking collectives  12.2 us (4%)
  local copies, waits for them, and re-layouts  11 us (4%)
    all_gather x1, waiting for transfers between devices, on_device(): gathered = lax.all_gather(scaled, 'rep', axis=0, tiled=True)  142 us
    all_gather x1, waiting for transfers between devices, on_device(): piece = lax.all_gather(grads, 'rack', axis=1, tiled=True)  36.5 us
    all_gather x1, waiting for transfers between devices, on_device(): lax.all_gather(right_root, 'rack', axis=1, tiled=True)  34.6 us
    reduce_scatter x1, waiting for transfers between devices, on_device(): lax.psum_scatter(jnp.einsum('sjr,sjk->rsk', grads, grads, preferred_eleme...  16 us
    psum x1, blocking collectives, on_device(): totals = lax.psum(partial_sums, 'rack')  12.2 us
    gather x1, local copies, waits for them, and re-layouts, on_device(): directions = jnp.take(gathered, place, axis=0)  11 us
    select_n x1, other arithmetic, on_device(): directions = jnp.take(gathered, place, axis=0)  7.65 us
  transfers between devices with their start and end apart: 4, of which 4 were waited for; matrix products, arithmetic and copies ran while one was open for 7% of the time, Pallas kernels for 0%

commit v1 on v0

v1 whole, which is shorter than its diff:
```python
import functools

import jax
import jax.numpy as jnp
from jax import lax
from jax.experimental import pallas as pl
from jax.experimental.pallas import tpu as pltpu
from jax.sharding import PartitionSpec as P

MESH = pl.DeviceIdType.MESH
BF, F32, I32 = jnp.bfloat16, jnp.float32, jnp.int32

NX, NY, NZ = 4, 4, 8
ROWS, WIDTH, SLOTS_DEV = 128, 1024, 2
HALF_A = 192
QUARTER = 160
HALF_B = QUARTER // 2
FIRST_B = 2 * HALF_A
CHUNK = HALF_A + HALF_B
OWN = SLOTS_DEV * NY
LAG = 3
LAG_Y = 3
SECOND = 12
STEPS = 46
KEEP = 8
ORDER = (
    (0, 0), (0, 1), (0, 2), (0, 3), (1, 0), (0, 4), (1, 1), (0, 5), (1, 2), (0, 6), (1, 3), (1, 4), (1, 5), (1, 6),
)


def me():
    rep, rack = lax.axis_index("rep"), lax.axis_index("rack")
    return rep // NY, rep % NY, rack // 2, rack % 2


def dev(z, y, x, c):
    return (z * NY + y, x * 2 + c)


def rcopy(src, dst, send, recv, to):
    return pltpu.make_async_remote_copy(
        src_ref=src, dst_ref=dst, send_sem=send, recv_sem=recv, device_id=to, device_id_type=MESH
    )


def schedule(owner_row, owner_col, z, y):
    row = lax.broadcasted_iota(I32, (8, 128), 0)
    lane = lax.broadcasted_iota(I32, (8, 128), 1)
    own = jnp.broadcast_to(owner_row, (8, 128))
    cnt = [
        jnp.broadcast_to(
            jnp.sum((own == row * NY + k).astype(I32), axis=1, keepdims=True), (8, 128)
        )
        for k in range(NY)
    ]
    used = [[(c > p).astype(I32) for c in cnt] for p in range(SLOTS_DEV)]
    size = [u[0] + u[1] + u[2] + u[3] for u in used]
    before = [[sum(u[:k], jnp.zeros((8, 128), I32)) for k in range(NY)] for u in used]
    start = []
    tables = []
    for turn in (1, -1):
        st = {}
        end = jnp.zeros((8, 128), I32)
        table = jnp.zeros((8, 128), I32)
        for p, d in ORDER:
            at = end
            if p == 1 and d == 0:
                at = jnp.maximum(at, SECOND)
            if d > 0:
                came = pltpu.roll(st[p, d - 1], turn % 8, 0)
                at = jnp.maximum(at, came + LAG)
            st[p, d] = at
            count = size[p] if d == 0 else pltpu.roll(size[p], (turn * d) % 8, 0)
            end = at + count
            spot = lane - at
            if d == 0:
                entry = jnp.zeros((8, 128), I32)
                for k in range(NY):
                    hit = (used[p][k] == 1) & (before[p][k] == spot)
                    entry = entry + jnp.where(hit, p * NY + k, 0)
            else:
                entry = OWN + came + spot
            table = jnp.where((lane >= at) & (lane < end), entry, table)
        start.append(st)
        tables.append(table)
    earlier = (owner_col == owner_row) & (
        lax.broadcasted_iota(I32, (32, 128), 0) < lax.broadcasted_iota(I32, (32, 128), 1)
    )
    slot = jnp.broadcast_to(jnp.sum(earlier.astype(I32), axis=0, keepdims=True), (8, 128))
    zb, yb = own >> 2, own & 3
    rank = jnp.zeros((8, 128), I32)
    for k in range(NY):
        line = jnp.sum((owner_col == (owner_row >> 2) * NY + k).astype(I32), axis=0, keepdims=True)
        line = jnp.broadcast_to(line, (8, 128))
        rank = rank + ((line > slot) & (yb > k)).astype(I32)
    found = []
    for way, turn in enumerate((1, -1)):
        hops = (turn * (z - zb)) & 7
        came_at = jnp.zeros((8, 128), I32)
        sender = (z - turn) & 7
        for p in range(SLOTS_DEV):
            for d in range(7):
                st = jnp.sum(jnp.where(row == sender, start[way][p, d], 0), axis=0, keepdims=True)
                came_at = jnp.where((hops == d + 1) & (slot == p), st + rank, came_at)
        found.append(jnp.minimum(came_at, STEPS - 1))
    here = (zb == z).astype(I32)
    mine = slot * NY + yb
    finds = jnp.where(row == 0, found[0], 0)
    finds = jnp.where(row == 1, found[1], finds)
    finds = jnp.where(row == 2, here, finds)
    finds = jnp.where(row == 3, mine, finds)
    finds = jnp.where(row == 4, zb, finds)
    finds = jnp.where(row == 5, yb, finds)
    finds = jnp.where(row == 6, slot, finds)
    held = jnp.sum((own == z * NY + y).astype(I32), axis=1, keepdims=True)
    return tables, finds, held[:1]


def main_kernel(
    grads, left, right, left_root, right_root, second, owner_row, owner_col,
    left_new, right_new, second_new, zout, nout, oout, lout, sout, finds_out,
    xb, lp, mixed, stack, ol, zland, pool, zst, yst, ynear, yopp,
    table_v, table_s, part, rk, ry, rz, tile,
    xsend, xrecv, osend, orecv, zsend, zrecv, nsend, nrecv, psend, precv,
    rsend, rrecv, sysend, syrecv, szsend, szrecv, lsem, outsem,
):
    z, y, x, c = me()
    rack = x * 2 + c
    xp, xm = dev(z, y, (x + 1) % NX, c), dev(z, y, (x + NX - 1) % NX, c)
    sibling = dev(z, y, x, 1 - c)
    ypeer = [None] + [dev(z, (y + k) % NY, x, c) for k in range(1, NY)]
    zpeer = [None] + [dev((z + k) % NZ, y, x, c) for k in range(1, NZ)]
    rpeer = [None] + [(z * NY + y, (rack + k) % 8) for k in range(1, 8)]
    yn = (ypeer[1], ypeer[3])
    zn = (zpeer[1], zpeer[7])

    barrier = pltpu.get_barrier_semaphore()
    peers = ypeer[1:] + zpeer[1:] + rpeer[1:]
    for p in peers:
        pl.semaphore_signal(barrier, inc=1, device_id=p, device_id_type=MESH)
    pl.semaphore_wait(barrier, len(peers))

    def source(w):
        return (grads, right_root)[w % 2].at[w // 2]

    def xrow(xx, lo, n):
        return pl.ds(pl.multiple_of((c * NX + xx) * ROWS + lo, 64), n)

    def x_copy(w, k):
        lo = (0, 64, 64, 0)[k] if k < 4 else (0, 64)[k - 4]
        if k < 4:
            src = source(w).at[lo : lo + 64]
            dst = xb.at[w, xrow(x, lo, 64)]
        else:
            frm = (x + NX - 1) % NX if k == 4 else (x + 1) % NX
            src = dst = xb.at[w, xrow(frm, lo, 64)]
        to = (xp, xp, xm, xm, xp, xm)[k]
        return rcopy(src, dst, xsend.at[w, k], xrecv.at[w, k], to)

    def core_copy(w):
        rows = xb.at[w, pl.ds(pl.multiple_of(c * 512, 512), 512)]
        return rcopy(rows, rows, xsend.at[w, 6], xrecv.at[w, 6], sibling)

    def x_own(w):
        for k in (0, 2, 1, 3):
            x_copy(w, k).start()
        xb[w, xrow(x, 0, ROWS), :] = source(w)[...]

    def x_forward(w):
        x_copy(w, 0).wait_recv()
        x_copy(w, 4).start()
        x_copy(w, 2).wait_recv()
        x_copy(w, 5).start()

    def x_rest(w):
        for k in (1, 3, 4, 5):
            x_copy(w, k).wait_recv()
        core_copy(w).start()

    def x_done(w):
        core_copy(w).wait_recv()

    def x_drain(w):
        for k in range(6):
            x_copy(w, k).wait_send()
        core_copy(w).wait_send()

    def mix(s):
        for k in range(8):
            to = (k % 2) * NX + k // 2
            lp[:, to * 128 : to * 128 + 128] = left_root[s, :, k * 128 : k * 128 + 128]
        for m in range(4):
            got = jnp.dot(lp[...], xb[2 * s, :, m * 256 : m * 256 + 256], preferred_element_type=F32)
            got = got.astype(BF)
            mixed[:, m * 128 : m * 128 + 128] = got[:, :128]
            mixed[:, 512 + m * 128 : 512 + m * 128 + 128] = got[:, 128:]

    def precondition(s):
        total = jnp.zeros((8, 128), F32)
        for m in range(4):
            got = jnp.dot(mixed[...], xb[2 * s + 1, :, m * 256 : m * 256 + 256], preferred_element_type=F32)
            got_b = got.astype(BF)
            stack[s, m * 256 : m * 256 + 128, :] = got_b[:, :128]
            stack[s, m * 256 + 128 : m * 256 + 256, :] = got_b[:, 128:]
            sq = got * got
            sq = sq[:, :128] + sq[:, 128:]
            total = total + jnp.sum(sq.reshape(16, 8, 128), axis=0)
        part[2 * s + 1] = total

    def factors(s, keep):
        for m in range(4):
            a, h = m // 2, m % 2
            outer = lax.dot_general(
                grads[s], xb[2 * s, m * 256 : m * 256 + 256, :], (((1,), (1,)), ((), ())),
                preferred_element_type=F32,
            )
            for i in range(2):
                col = ((2 * h + i) * 2 + a) * 128
                old = left[s, :, col : col + 128]
                old = old.astype(F32)
                new = 0.95 * old + 0.05 * outer[:, i * 128 : i * 128 + 128]
                left_new[s, :, col : col + 128] = jnp.where(keep, new, old).astype(BF)
        mine = xb[2 * s, :, pl.ds(pl.multiple_of(rack * 128, 128), 128)]
        for m in range(4):
            cols = slice(m * 256, m * 256 + 256)
            inner = lax.dot_general(
                mine, xb[2 * s, :, cols], (((0,), (0,)), ((), ())), preferred_element_type=F32
            )
            old = right[s, :, cols].astype(F32)
            new = 0.95 * old + 0.05 * inner
            right_new[s, :, cols] = jnp.where(keep, new, old).astype(BF)

    def graft(s, keep):
        def tile_rows(i, total):
            rows = pl.ds(pl.multiple_of(i * 16, 16), 16)
            g = grads[s, rows, :].astype(F32)
            old = second[s, rows, :].astype(F32)
            moment = 0.95 * old + 0.05 * g * g
            second_new[s, rows, :] = jnp.where(keep, moment, old).astype(BF)
            adam = g / (jnp.sqrt(moment) + 1e-8)
            return total + adam * adam

        total = lax.fori_loop(0, 8, tile_rows, jnp.zeros((16, WIDTH), F32))
        total = jnp.sum(total.reshape(2, 8, WIDTH), axis=0)
        acc = total[:, :128]
        for k in range(1, 8):
            acc = acc + total[:, k * 128 : k * 128 + 128]
        part[2 * s] = acc

    def quarter(k):
        return pl.ds(pl.multiple_of(FIRST_B + QUARTER * k, 16), QUARTER)

    def line_copy(s, k, i):
        to = (y + k) % NY
        rows = pl.ds(0, FIRST_B) if i == 0 else quarter((to + i - 1) % NY)
        return rcopy(
            stack.at[s, rows], ol.at[s * NY + y, rows], osend.at[s, k - 1, i], orecv.at[s, k - 1, i], ypeer[k]
        )

    def line_recv(s, k, i):
        frm = (y + NY - k) % NY
        rows = pl.ds(0, FIRST_B) if i == 0 else quarter((y + i - 1) % NY)
        return rcopy(
            stack.at[s, rows], ol.at[s * NY + frm, rows], osend.at[s, k - 1, i], orecv.at[s, k - 1, i], ypeer[k]
        )

    def line_first(s):
        for i in (0, 1):
            for k in (1, 3, 2):
                line_copy(s, k, i).start()
        ol[pl.ds(s * NY + y, 1)] = stack[s][None]

    def line_second(s):
        for i in (2, 3, 4):
            for k in (1, 3, 2):
                line_copy(s, k, i).start()

    def line_pool(s):
        for i in (0, 1):
            for k in (1, 3, 2):
                line_recv(s, k, i).wait_recv()
        for k in range(NY):
            e = s * NY + k
            for way in range(2):
                pool[way, e, :HALF_A] = ol[e, way * HALF_A : way * HALF_A + HALF_A, :]
                lo = pl.multiple_of(FIRST_B + QUARTER * y + way * HALF_B, 16)
                pool[way, e, HALF_A:] = ol[e, pl.ds(lo, HALF_B), :]

    def z_copy(way, t):
        return rcopy(
            zst.at[way, t % KEEP], zland.at[way, t], zsend.at[way, t % KEEP], zrecv.at[way, t], zn[way]
        )

    def n_copy(way, t):
        return rcopy(yst.at[t], ynear.at[way, t], nsend.at[way, t % KEEP], nrecv.at[way, t], yn[way])

    def p_copy(way, t):
        return rcopy(
            ynear.at[way, t, pl.ds(way * HALF_B, HALF_B)], yopp.at[way, t],
            psend.at[way, t % KEEP], precv.at[way, t], yn[way],
        )

    def z_send(t, again):
        for way in range(2):
            if again:
                z_copy(way, t - KEEP).wait_send()
            zst[way, t % KEEP] = pool[way, table_s[way, z, t]]
            z_copy(way, t).start()

    def z_take(t, again):
        for way in range(2):
            z_copy(way, t).wait_recv()
            pool[way, OWN + t] = zland[way, t]
            yst[t, way * HALF_B : way * HALF_B + HALF_B, :] = zland[way, t, HALF_A:, :]
        for way in range(2):
            if again:
                n_copy(way, t - KEEP).wait_send()
            n_copy(way, t).start()

    def y_take(t, again):
        for way in range(2):
            n_copy(way, t).wait_recv()
            if again:
                p_copy(way, t - KEEP).wait_send()
            p_copy(way, t).start()

    marks = sorted({0, LAG, LAG + LAG_Y, KEEP, KEEP + LAG, KEEP + LAG + LAG_Y, STEPS, STEPS + LAG, STEPS + LAG + LAG_Y})

    def steps(a, b):
        cuts = [a] + [k for k in marks if a < k < b] + [b]
        for lo, hi in zip(cuts[:-1], cuts[1:]):
            def body(t, _, lo=lo):
                if LAG <= lo < STEPS + LAG:
                    z_take(t - LAG, lo - LAG >= KEEP)
                if lo < STEPS:
                    z_send(t, lo >= KEEP)
                if LAG + LAG_Y <= lo < STEPS + LAG + LAG_Y:
                    y_take(t - LAG - LAG_Y, lo - LAG - LAG_Y >= KEEP)
                return 0

            lax.fori_loop(lo, hi, body, 0)

    def r_copy(k):
        return rcopy(tile.at[0], rk.at[k], rsend.at[k - 1], rrecv.at[k - 1], rpeer[k])

    def sy_copy(k):
        return rcopy(tile.at[1], ry.at[y], sysend.at[k - 1], syrecv.at[k - 1], ypeer[k])

    def sz_copy(k):
        return rcopy(ry, rz.at[z], szsend.at[k - 1], szrecv.at[k - 1], zpeer[k])

    sub = lax.broadcasted_iota(I32, (8, 128), 0)

    def scale_first():
        own = jnp.zeros((8, 128), F32)
        for i in range(4):
            whole = jnp.sum(jnp.sum(part[i], axis=0, keepdims=True), axis=1, keepdims=True)
            own = jnp.where(sub == i, jnp.broadcast_to(whole, (8, 128)), own)
        tile[0] = own
        rk[0] = own
        for k in range(1, 8):
            r_copy(k).start()

    def scale_second():
        for k in range(1, 8):
            r_copy(k).wait_recv()
        total = rk[0]
        for k in range(1, 8):
            total = total + rk[k]
        out = jnp.zeros((8, 128), F32)
        for s in range(2):
            value = jnp.sqrt(total[2 * s : 2 * s + 1]) / jnp.sqrt(total[2 * s + 1 : 2 * s + 2] + 1e-6)
            out = jnp.where(sub == s, jnp.broadcast_to(value, (8, 128)), out)
        tile[1] = out
        ry[pl.ds(y, 1)] = out[None]
        for k in range(1, 4):
            sy_copy(k).start()

    def sy_recv(k):
        frm = (y + NY - k) % NY
        return rcopy(tile.at[1], ry.at[frm], sysend.at[k - 1], syrecv.at[k - 1], ypeer[k])

    def sz_recv(k):
        frm = (z + NZ - k) % NZ
        return rcopy(ry, rz.at[frm], szsend.at[k - 1], szrecv.at[k - 1], zpeer[k])

    def scale_third():
        for k in range(1, 4):
            sy_recv(k).wait_recv()
        rz[pl.ds(z, 1)] = ry[...][None]
        for k in range(1, 8):
            sz_copy(k).start()

    x_own(0)
    tables, finds, held = schedule(owner_row[...], owner_col[...], z, y)
    for way in range(2):
        table_v[way] = tables[way]
    finds_out[...] = finds
    to_smem = pltpu.make_async_copy(table_v, table_s, lsem.at[0])
    to_smem.start()
    x_forward(0)
    x_own(1)
    graft(0, held > 0)
    graft(1, held > 1)
    x_rest(0)
    x_forward(1)
    x_own(2)
    x_done(0)
    mix(0)
    x_rest(1)
    x_forward(2)
    x_own(3)
    x_done(1)
    precondition(0)
    line_first(0)
    factors(0, held > 0)
    to_smem.wait()
    line_pool(0)
    steps(0, 2)
    line_second(0)
    x_rest(2)
    x_forward(3)
    steps(2, 4)
    x_done(2)
    mix(1)
    steps(4, 6)
    x_rest(3)
    steps(6, 8)
    x_done(3)
    precondition(1)
    line_first(1)
    scale_first()
    steps(8, SECOND)
    line_pool(1)
    steps(SECOND, SECOND + 3)
    line_second(1)
    scale_second()
    factors(1, held > 1)
    steps(SECOND + 3, SECOND + 8)
    scale_third()
    steps(SECOND + 8, STEPS + LAG + LAG_Y)

    def put(i, src, dst):
        return pltpu.make_async_copy(src, dst, outsem.at[i])

    puts = [put(0, zland, zout), put(1, ynear, nout)]
    for p in puts:
        p.start()
    for s in range(2):
        for i in (2, 3, 4):
            for k in (1, 3, 2):
                line_recv(s, k, i).wait_recv()
    more = [put(2, ol, lout)]
    more[0].start()
    for k in range(1, 8):
        sz_recv(k).wait_recv()
    more.append(put(3, rz, sout))
    more[1].start()
    for t in range(STEPS):
        for way in range(2):
            p_copy(way, t).wait_recv()
    more.append(put(4, yopp, oout))
    more[2].start()
    for w in range(4):
        x_drain(w)
    for s in range(2):
        for k in range(1, 4):
            for i in range(5):
                line_copy(s, k, i).wait_send()
    for t in range(STEPS - KEEP, STEPS):
        for way in range(2):
            z_copy(way, t).wait_send()
            n_copy(way, t).wait_send()
            p_copy(way, t).wait_send()
    for k in range(1, 8):
        r_copy(k).wait_send()
        sz_copy(k).wait_send()
    for k in range(1, 4):
        sy_copy(k).wait_send()
    for p in puts + more:
        p.wait()


def spread_kernel(finds, zp, near, opp, line, scales, out, zv, nv, ov, lv, sv, flat, rows_out, insem, outsem):
    _, y, _, _ = me()
    pairs = [(zp, zv), (near, nv), (opp, ov), (line, lv), (scales, sv)]
    loads = [pltpu.make_async_copy(a, b, insem.at[i]) for i, (a, b) in enumerate(pairs)]
    for k in loads:
        k.start()
    for k in loads:
        k.wait()

    def store(b, src):
        keep = b % 4
        scale = sv[finds[4, b], finds[5, b], pl.ds(finds[6, b], 1), :]

        @pl.when(b >= 4)
        def _():
            pltpu.make_async_copy(rows_out.at[keep], out.at[b - 4], outsem.at[keep]).wait()

        for col in range(8):
            part = src(col).astype(F32) * scale
            rows_out[keep, :, col * 128 : col * 128 + 128] = part.astype(BF)
        pltpu.make_async_copy(rows_out.at[keep], out.at[b], outsem.at[keep]).start()

    def one(b, _):
        tp, tm = finds[0, b], finds[1, b]

        @pl.when(finds[2, b] == 1)
        def _():
            e = finds[3, b]
            store(b, lambda col: lv[e, col * 128 : col * 128 + 128, :])

        @pl.when(finds[2, b] == 0)
        def _():
            flat[:HALF_A] = zv[0, tp, :HALF_A]
            flat[HALF_A : 2 * HALF_A] = zv[1, tm, :HALF_A]

            def quarter(q, plus, minus):
                lo = pl.multiple_of(FIRST_B + QUARTER * (q % NY), 16)
                flat[pl.ds(lo, HALF_B)] = plus
                flat[pl.ds(pl.multiple_of(lo + HALF_B, 16), HALF_B)] = minus

            quarter(y, zv[0, tp, HALF_A:], zv[1, tm, HALF_A:])
            quarter(y + NY - 1, nv[0, tp, :HALF_B], nv[0, tm, HALF_B:])
            quarter(y + 1, nv[1, tp, :HALF_B], nv[1, tm, HALF_B:])
            quarter(y + 2, ov[0, tp], ov[1, tm])
            store(b, lambda col: flat[col * 128 : col * 128 + 128])

        return 0

    lax.fori_loop(0, 32, one, 0)
    for b in range(28, 32):
        pltpu.make_async_copy(rows_out.at[b % 4], out.at[b], outsem.at[b % 4]).wait()


def on_device(grads, left, right, left_root, right_root, second, owner):
    owner_row = jnp.pad(owner, (0, 128 - owner.shape[0]), constant_values=-1).reshape(1, 128)
    owner_col = jnp.broadcast_to(owner[:, None], (32, 128))
    vmem, hbm = pl.BlockSpec(memory_space=pltpu.VMEM), pl.BlockSpec(memory_space=pl.ANY)
    shape = jax.ShapeDtypeStruct
    block = shape((SLOTS_DEV, ROWS, WIDTH), BF)
    z_shape, n_shape, o_shape = (2, STEPS, CHUNK, 128), (2, STEPS, QUARTER, 128), (2, STEPS, HALF_B, 128)
    l_shape, s_shape = (OWN, WIDTH, 128), (NZ, NY, 8, 128)
    dma = pltpu.SemaphoreType.DMA
    left_new, right_new, second_new, zp, near, opp, line, scales, finds = pl.pallas_call(
        main_kernel,
        out_shape=(
            block, block, block, shape(z_shape, BF), shape(n_shape, BF), shape(o_shape, BF), shape(l_shape, BF),
            shape(s_shape, F32), shape((8, 128), I32),
        ),
        in_specs=[vmem] * 8,
        out_specs=(vmem, vmem, vmem, hbm, hbm, hbm, hbm, hbm, vmem),
        scratch_shapes=[
            pltpu.VMEM((4, WIDTH, WIDTH), BF),
            pltpu.VMEM((ROWS, WIDTH), BF),
            pltpu.VMEM((ROWS, WIDTH), BF),
            pltpu.VMEM((SLOTS_DEV, WIDTH, 128), BF),
            pltpu.VMEM(l_shape, BF),
            pltpu.VMEM(z_shape, BF),
            pltpu.VMEM((2, OWN + STEPS, CHUNK, 128), BF),
            pltpu.VMEM((2, KEEP, CHUNK, 128), BF),
            pltpu.VMEM((STEPS, QUARTER, 128), BF),
            pltpu.VMEM(n_shape, BF),
            pltpu.VMEM(o_shape, BF),
            pltpu.VMEM((2, 8, 128), I32),
            pltpu.SMEM((2, 8, 128), I32),
            pltpu.VMEM((4, 8, 128), F32),
            pltpu.VMEM((8, 8, 128), F32),
            pltpu.VMEM((NY, 8, 128), F32),
            pltpu.VMEM(s_shape, F32),
            pltpu.VMEM((2, 8, 128), F32),
            dma((4, 7)), dma((4, 7)),
            dma((2, 3, 5)), dma((2, 3, 5)),
            dma((2, KEEP)), dma((2, STEPS)),
            dma((2, KEEP)), dma((2, STEPS)),
            dma((2, KEEP)), dma((2, STEPS)),
            dma((7,)), dma((7,)), dma((3,)), dma((3,)), dma((7,)), dma((7,)),
            dma((1,)), dma((5,)),
        ],
        compiler_params=pltpu.CompilerParams(
            collective_id=1, has_side_effects=True, vmem_limit_bytes=56 << 20
        ),
        name="shampoo",
    )(grads, left, right, left_root, right_root, second, owner_row, owner_col)
    directions = pl.pallas_call(
        spread_kernel,
        out_shape=shape((32, ROWS, WIDTH), BF),
        in_specs=[pl.BlockSpec(memory_space=pltpu.SMEM)] + [hbm] * 5,
        out_specs=hbm,
        scratch_shapes=[
            pltpu.VMEM(z_shape, BF), pltpu.VMEM(n_shape, BF), pltpu.VMEM(o_shape, BF), pltpu.VMEM(l_shape, BF),
            pltpu.VMEM(s_shape, F32),
            pltpu.VMEM((WIDTH, 128), BF),
            pltpu.VMEM((4, ROWS, WIDTH), BF),
            dma((5,)), dma((4,)),
        ],
        compiler_params=pltpu.CompilerParams(vmem_limit_bytes=48 << 20),
        name="spread",
    )(finds, zp, near, opp, line, scales)
    return (left_new, right_new, second_new, directions)


def solution(mesh):
    block = P("rep", "rack", None)
    return jax.shard_map(
        on_device,
        mesh=mesh,
        in_specs=(block,) * 6 + (P(),),
        out_specs=(block, block, block, P(None, "rack", None)),
        check_vma=False,
    )
```

time: 296 us -> 160 us (0.54)
  waiting for transfers between devices: 231 us -> 0 us
  Pallas kernels: 0 us -> 147 us
  matrix products: 14.1 us -> 0 us
  other arithmetic: 13.4 us -> 0 us
  between operations: 13.9 us -> 0.67 us
  blocking collectives: 12.2 us -> 0 us
    all_gather x3 -> x0, waiting for transfers between devices: 213 us -> none  [the longest x1 142 us: on_device(): gathered = lax.all_gather(scaled, 'rep', axis=0, tiled=True)]
    pallas_call x0 -> x2, Pallas kernels: none -> 147 us  [the longest x1 136 us: on_device(): pl.pallas_call(main_kernel, out_shape=(block, block, block, shape(z_shape...]
    reduce_scatter x1 -> x0, waiting for transfers between devices: 16 us -> none  [on_device(): lax.psum_scatter(jnp.einsum('sjr,sjk->rsk', grads, grads, preferred_eleme...]
    dot_general x3 -> x0, matrix products: 14.1 us -> none  [the longest x1 4.86 us: on_device(): jnp.einsum('srn,snk->srk', mixed_b, lax.all_gather(right_root, 'rack', ax...]
    psum x1 -> x0, blocking collectives: 12.2 us -> none  [on_device(): totals = lax.psum(partial_sums, 'rack')]
    gather x1 -> x0, local copies, waits for them, and re-layouts: 11 us -> none  [on_device(): directions = jnp.take(gathered, place, axis=0)]
    select_n x2 -> x0, other arithmetic: 10.2 us -> none  [the longest x1 7.65 us: on_device(): directions = jnp.take(gathered, place, axis=0)]
    unnamed x12 -> x17, local copies, waits for them, and re-layouts: 0.03 us -> 7.07 us
  transfers between devices with their start and end apart: 4 -> 0, of which waited for: 4 -> 0; matrix products, arithmetic and copies ran while one was open for 7% -> 0% of each run, Pallas kernels for 0% -> 0%
where the time goes in v1:
time: 160 us; the launch traced here: 157 us
  Pallas kernels  147 us (92%)
  local copies, waits for them, and re-layouts  9.57 us (6%)
    pallas_call x1, Pallas kernels, on_device(): pl.pallas_call(main_kernel, out_shape=(block, block, block, shape(z_shape...  136 us
    pallas_call x1, Pallas kernels, on_device(): pl.pallas_call(spread_kernel, out_shape=shape((32, ROWS, WIDTH), BF), in_...  11.1 us
    unnamed x17, local copies, waits for them, and re-layouts  7.07 us

profile of v1, /device:TPU:1, one launch (start us, length us, event | category | flops | bytes accessed | tf_op | source)
XLA Modules:
  0.0 157.3 jit_solution(9418423192200637229)
XLA Ops:
  0.6 1.2 pad_bitcast_fusion.owner_row
  1.8 1.3 broadcast_in_dim.2.owner_col
  3.1 135.9 %shampoo.1 = (bf16[2,128,1024]{2,1,0:T(8,128)(2,1)}, bf16[2,128,1024]{2,1,0:T(8,128)(2,1)}, bf16[2,128,1024]{2,1,0:T(8,128)(2,1)}, bf16[2,46,272,128]{3,2,1,0:T(...) custom-call(bf16[2,128,1024]{2,1,0:T(8,128)(2,1)} %grads.1, ...), custom_call_target="tpu_custom_call" | custom-call | tf_op jit(solution)/shard_map/shampoo/pallas_call | solution.py:546
  139.0 0.0 copy-start
  139.1 1.6 %copy-done = bf16[8,1024,128]{2,1,0:T(8,128)(2,1)S(1)} copy-done((bf16[8,1024,128]{2,1,0:T(8,128)(2,1)S(1)}, bf16[8,1024,128]{2,1,0:T(8,128)(2,1)}, u32[]{:S(2)}) %copy-start) | copy-done | bytes 2097176
  140.6 0.0 copy-start.1
  140.6 1.5 copy-done.1
  142.2 0.0 copy-start.2
  142.2 0.9 copy-done.2
  143.1 0.0 copy-start.3
  143.1 0.7 copy-done.3
  143.7 0.0 copy-start.6
  143.7 0.0 copy-start.5
  143.7 0.0 copy-start.4
  143.7 11.1 %spread.1 = bf16[32,128,1024]{2,1,0:T(8,128)(2,1)} custom-call(s32[8,128]{1,0:T(8,128)S(1)} %copy-done.3, bf16[2,46,272,128]{3,2,1,0:T(8,128)(2,1)} %get-tuple-element.17.zp, bf16[2,46,160,128]{3,2,1,0:T(8,128)(2,1)} %get-tuple-element.18.near, bf16[2,46,80,128]{3,2,1,0:T(8,128)(2,1)S(1)} %copy-done.1, bf16[8,1024,128]{2,1,0:T(8,128)(2,1)S(1)} %copy-done, ...), custom_call_target="tpu_custom_call" | custom-call | tf_op jit(solution)/shard_map/spread/pallas_call | solution.py:586
  154.9 0.0 copy-done.6
  154.9 0.8 copy.14
  155.7 0.0 copy-done.5
  155.7 0.8 copy.15
  156.5 0.0 copy-done.4
  156.5 0.8 copy.16
Async XLA Ops:
  139.0 1.6 %copy-start = (bf16[8,1024,128]{2,1,0:T(8,128)(2,1)S(1)}, bf16[8,1024,128]{2,1,0:T(8,128)(2,1)}, u32[]{:S(2)}) copy-start(bf16[8,1024,128]{2,1,0:T(8,128)(2,1)} %get-tuple-element.20.line) | copy-start | bytes 6291460
  140.6 1.5 copy-start.1
  142.2 0.9 copy-start.2
  143.1 0.7 copy-start.3
  143.7 11.1 %copy-start.6 = (bf16[2,128,1024]{2,1,0:T(8,128)(2,1)S(1)}, bf16[2,128,1024]{2,1,0:T(8,128)(2,1)}, u32[]{:S(2)}) copy-start(bf16[2,128,1024]{2,1,0:T(8,128)(2,1)} %get-tuple-element.26) | copy-start | bytes 1572868
  143.7 11.9 %copy-start.5 = (bf16[2,128,1024]{2,1,0:T(8,128)(2,1)S(1)}, bf16[2,128,1024]{2,1,0:T(8,128)(2,1)}, u32[]{:S(2)}) copy-start(bf16[2,128,1024]{2,1,0:T(8,128)(2,1)} %get-tuple-element.27) | copy-start | bytes 1572868
  143.7 12.7 %copy-start.4 = (bf16[2,128,1024]{2,1,0:T(8,128)(2,1)S(1)}, bf16[2,128,1024]{2,1,0:T(8,128)(2,1)}, u32[]{:S(2)}) copy-start(bf16[2,128,1024]{2,1,0:T(8,128)(2,1)} %get-tuple-element.28) | copy-start | bytes 1572868

commit v2 on v1

--- a/solution.py
+++ b/solution.py
@@ -19,12 +19,12 @@
 CHUNK = HALF_A + HALF_B
 OWN = SLOTS_DEV * NY
 LAG = 3
-LAG_Y = 3
-SECOND = 12
-STEPS = 46
+LAG_Y = 5
+SECOND = 10
+STEPS = 44
 KEEP = 8
 ORDER = (
-    (0, 0), (0, 1), (0, 2), (0, 3), (1, 0), (0, 4), (1, 1), (0, 5), (1, 2), (0, 6), (1, 3), (1, 4), (1, 5), (1, 6),
+    (0, 0), (0, 1), (0, 2), (1, 0), (0, 3), (1, 1), (0, 4), (1, 2), (0, 5), (1, 3), (0, 6), (1, 4), (1, 5), (1, 6),
 )
 
 
@@ -43,10 +43,16 @@
     )
 
 
-def schedule(owner_row, owner_col, z, y):
+def schedule(owner, z, y):
     row = lax.broadcasted_iota(I32, (8, 128), 0)
     lane = lax.broadcasted_iota(I32, (8, 128), 1)
-    own = jnp.broadcast_to(owner_row, (8, 128))
+    own = jnp.full((8, 128), -1, I32)
+    owner_col = jnp.zeros((32, 128), I32)
+    sub = lax.broadcasted_iota(I32, (32, 128), 0)
+    for b in range(32):
+        own = jnp.where(lane == b, owner[b], own)
+        owner_col = jnp.where(sub == b, owner[b], owner_col)
+    owner_row = own[:1]
     cnt = [
         jnp.broadcast_to(
             jnp.sum((own == row * NY + k).astype(I32), axis=1, keepdims=True), (8, 128)
@@ -117,12 +123,12 @@
 
 
 def main_kernel(
-    grads, left, right, left_root, right_root, second, owner_row, owner_col,
-    left_new, right_new, second_new, zout, nout, oout, lout, sout, finds_out,
-    xb, lp, mixed, stack, ol, zland, pool, zst, yst, ynear, yopp,
+    grads_h, left_h, right_h, left_root_h, right_root_h, second_h, owner,
+    left_o, right_o, second_o, zout, nout, oout, lout, sout, finds_o,
+    grads, left, right, left_root, second, left_new, right_new, second_new, finds_out, xb, mixed, stack, ol, zland, pool, zst, yst, ynear, yopp,
     table_v, table_s, part, rk, ry, rz, tile,
     xsend, xrecv, osend, orecv, zsend, zrecv, nsend, nrecv, psend, precv,
-    rsend, rrecv, sysend, syrecv, szsend, szrecv, lsem, outsem,
+    rsend, rrecv, sysend, syrecv, szsend, szrecv, lsem, insem, outsem,
 ):
     z, y, x, c = me()
     rack = x * 2 + c
@@ -140,86 +146,105 @@
         pl.semaphore_signal(barrier, inc=1, device_id=p, device_id_type=MESH)
     pl.semaphore_wait(barrier, len(peers))
 
+    after, two, prior = (x + 1) % NX, (x + 2) % NX, (x + 3) % NX
+
     def source(w):
-        return (grads, right_root)[w % 2].at[w // 2]
-
-    def xrow(xx, lo, n):
-        return pl.ds(pl.multiple_of((c * NX + xx) * ROWS + lo, 64), n)
+        return (grads_h, right_root_h)[w % 2].at[w // 2]
+
+    def brow(xx, cc, lo=0, n=ROWS):
+        return pl.ds(pl.multiple_of((xx * 2 + cc) * ROWS + lo, 64), n)
+
+    def bcol(xx):
+        return pl.ds(pl.multiple_of(xx * 256, 256), 256)
 
     def x_copy(w, k):
-        lo = (0, 64, 64, 0)[k] if k < 4 else (0, 64)[k - 4]
-        if k < 4:
-            src = source(w).at[lo : lo + 64]
-            dst = xb.at[w, xrow(x, lo, 64)]
+        if w % 2 == 0:
+            lo = (0, 64, 64, 0, 0, 64)[k]
+            to = (xp, xp, xm, xm, xp, xm)[k]
+            if k < 4:
+                src, dst = source(w).at[lo : lo + 64], xb.at[w, brow(x, c, lo, 64)]
+            else:
+                src = dst = xb.at[w, brow(prior if k == 4 else after, c, lo, 64)]
         else:
-            frm = (x + NX - 1) % NX if k == 4 else (x + 1) % NX
-            src = dst = xb.at[w, xrow(frm, lo, 64)]
-        to = (xp, xp, xm, xm, xp, xm)[k]
+            to = (xp, xp, xp, xm, xm, xm)[k]
+            col = bcol((x, prior, two, x, after, after)[k])
+            if k < 5:
+                src, dst = source(w).at[:, col], xb.at[w, brow(x, c), col]
+            else:
+                src = dst = xb.at[w, brow(after, c), col]
         return rcopy(src, dst, xsend.at[w, k], xrecv.at[w, k], to)
 
-    def core_copy(w):
-        rows = xb.at[w, pl.ds(pl.multiple_of(c * 512, 512), 512)]
-        return rcopy(rows, rows, xsend.at[w, 6], xrecv.at[w, 6], sibling)
+    def core_copy(w, i):
+        rows = brow((x, prior, after, two)[i], c)
+        src = source(w) if i == 0 else xb.at[w, rows]
+        return rcopy(src, xb.at[w, rows], xsend.at[w, 6 + i], xrecv.at[w, 6 + i], sibling)
+
+    def own_copy(w):
+        return pltpu.make_async_copy(source(w), xb.at[w, brow(x, c)], insem.at[w])
 
     def x_own(w):
-        for k in (0, 2, 1, 3):
+        for k in ((0, 2, 1, 3), (3, 0, 4, 1, 2))[w % 2]:
             x_copy(w, k).start()
-        xb[w, xrow(x, 0, ROWS), :] = source(w)[...]
+        core_copy(w, 0).start()
+        own_copy(w).start()
 
     def x_forward(w):
-        x_copy(w, 0).wait_recv()
-        x_copy(w, 4).start()
-        x_copy(w, 2).wait_recv()
-        x_copy(w, 5).start()
+        for k, on in (((0, 4), (2, 5)), ((3, 5),))[w % 2]:
+            x_copy(w, k).wait_recv()
+            x_copy(w, on).start()
 
     def x_rest(w):
-        for k in (1, 3, 4, 5):
-            x_copy(w, k).wait_recv()
-        core_copy(w).start()
+        for i, ks in enumerate((((1,), (3,), (4, 5)), ((0, 1, 2), (4,), (5,)))[w % 2]):
+            for k in ks:
+                x_copy(w, k).wait_recv()
+            core_copy(w, 1 + i).start()
+
+    def x_held(w):
+        own_copy(w).wait()
+        core_copy(w, 0).wait_recv()
 
     def x_done(w):
-        core_copy(w).wait_recv()
+        for i in range(1, 4):
+            core_copy(w, i).wait_recv()
 
     def x_drain(w):
         for k in range(6):
             x_copy(w, k).wait_send()
-        core_copy(w).wait_send()
+        for i in range(4):
+            core_copy(w, i).wait_send()
 
     def mix(s):
-        for k in range(8):
-            to = (k % 2) * NX + k // 2
-            lp[:, to * 128 : to * 128 + 128] = left_root[s, :, k * 128 : k * 128 + 128]
         for m in range(4):
-            got = jnp.dot(lp[...], xb[2 * s, :, m * 256 : m * 256 + 256], preferred_element_type=F32)
-            got = got.astype(BF)
-            mixed[:, m * 128 : m * 128 + 128] = got[:, :128]
-            mixed[:, 512 + m * 128 : 512 + m * 128 + 128] = got[:, 128:]
-
-    def precondition(s):
-        total = jnp.zeros((8, 128), F32)
-        for m in range(4):
-            got = jnp.dot(mixed[...], xb[2 * s + 1, :, m * 256 : m * 256 + 256], preferred_element_type=F32)
-            got_b = got.astype(BF)
-            stack[s, m * 256 : m * 256 + 128, :] = got_b[:, :128]
-            stack[s, m * 256 + 128 : m * 256 + 256, :] = got_b[:, 128:]
-            sq = got * got
-            sq = sq[:, :128] + sq[:, 128:]
-            total = total + jnp.sum(sq.reshape(16, 8, 128), axis=0)
-        part[2 * s + 1] = total
+            cols = slice(m * 256, m * 256 + 256)
+            mixed[:, cols] = jnp.dot(left_root[s], xb[2 * s, :, cols], preferred_element_type=F32).astype(BF)
+
+    def precondition(s, j):
+        w = 2 * s + 1
+        at = ((x, after, two, prior)[j]) * 256
+        got = jnp.zeros((ROWS, 256), F32)
+        for i in range(4):
+            lhs = mixed[:, bcol((x + i) % NX)]
+            here = i == 0 or (i, j) in ((3, 1), (3, 2), (3, 3), (1, 1), (1, 2), (2, 2))
+            r, k = (i, j) if here else (j, i)
+            block = xb[w, bcol((x + r) % NX), bcol((x + k) % NX)]
+            got += lax.dot_general(
+                lhs, block, (((1,), (0 if here else 1,)), ((), ())), preferred_element_type=F32
+            )
+        got_b = got.astype(BF)
+        stack[s, pl.ds(pl.multiple_of(at, 256), 128), :] = got_b[:, :128]
+        stack[s, pl.ds(pl.multiple_of(at + 128, 128), 128), :] = got_b[:, 128:]
+        sq = got * got
+        sq = jnp.sum((sq[:, :128] + sq[:, 128:]).reshape(16, 8, 128), axis=0)
+        part[2 * s + 1] = sq if j == 0 else part[2 * s + 1] + sq
 
     def factors(s, keep):
         for m in range(4):
-            a, h = m // 2, m % 2
+            cols = slice(m * 256, m * 256 + 256)
             outer = lax.dot_general(
-                grads[s], xb[2 * s, m * 256 : m * 256 + 256, :], (((1,), (1,)), ((), ())),
-                preferred_element_type=F32,
+                grads[s], xb[2 * s, cols, :], (((1,), (1,)), ((), ())), preferred_element_type=F32
             )
-            for i in range(2):
-                col = ((2 * h + i) * 2 + a) * 128
-                old = left[s, :, col : col + 128]
-                old = old.astype(F32)
-                new = 0.95 * old + 0.05 * outer[:, i * 128 : i * 128 + 128]
-                left_new[s, :, col : col + 128] = jnp.where(keep, new, old).astype(BF)
+            old = left[s, :, cols].astype(F32)
+            left_new[s, :, cols] = jnp.where(keep, 0.95 * old + 0.05 * outer, old).astype(BF)
         mine = xb[2 * s, :, pl.ds(pl.multiple_of(rack * 128, 128), 128)]
         for m in range(4):
             cols = slice(m * 256, m * 256 + 256)
@@ -307,10 +332,13 @@
             zst[way, t % KEEP] = pool[way, table_s[way, z, t]]
             z_copy(way, t).start()
 
-    def z_take(t, again):
+    def z_take(t):
         for way in range(2):
             z_copy(way, t).wait_recv()
             pool[way, OWN + t] = zland[way, t]
+
+    def y_send(t, again):
+        for way in range(2):
             yst[t, way * HALF_B : way * HALF_B + HALF_B, :] = zland[way, t, HALF_A:, :]
         for way in range(2):
             if again:
@@ -331,9 +359,11 @@
         for lo, hi in zip(cuts[:-1], cuts[1:]):
             def body(t, _, lo=lo):
                 if LAG <= lo < STEPS + LAG:
-                    z_take(t - LAG, lo - LAG >= KEEP)
+                    z_take(t - LAG)
                 if lo < STEPS:
                     z_send(t, lo >= KEEP)
+                if LAG <= lo < STEPS + LAG:
+                    y_send(t - LAG, lo - LAG >= KEEP)
                 if LAG + LAG_Y <= lo < STEPS + LAG + LAG_Y:
                     y_take(t - LAG - LAG_Y, lo - LAG - LAG_Y >= KEEP)
                 return 0
@@ -391,8 +421,25 @@
         for k in range(1, 8):
             sz_copy(k).start()
 
+    def put(i, src, dst):
+        copy = pltpu.make_async_copy(src, dst, outsem.at[i])
+        copy.start()
+        puts.append(copy)
+
+    def put_steps(lo, hi, i):
+        put(i, zland.at[:, lo:hi], zout.at[:, lo:hi])
+
+    puts = []
     x_own(0)
-    tables, finds, held = schedule(owner_row[...], owner_col[...], z, y)
+    loads = [
+        pltpu.make_async_copy(src, dst, insem.at[4 + i])
+        for i, (src, dst) in enumerate(
+            [(grads_h, grads), (left_root_h, left_root), (second_h, second), (left_h, left), (right_h, right)]
+        )
+    ]
+    for k in loads:
+        k.start()
+    tables, finds, held = schedule(owner, z, y)
     for way in range(2):
         table_v[way] = tables[way]
     finds_out[...] = finds
@@ -400,67 +447,80 @@
     to_smem.start()
     x_forward(0)
     x_own(1)
+    for k in loads:
+        k.wait()
+    put(0, finds_out, finds_o)
     graft(0, held > 0)
     graft(1, held > 1)
+    put(1, second_new, second_o)
     x_rest(0)
     x_forward(1)
     x_own(2)
+    x_held(0)
     x_done(0)
     mix(0)
+    x_held(1)
+    precondition(0, 0)
     x_rest(1)
     x_forward(2)
     x_own(3)
     x_done(1)
-    precondition(0)
+    for j in (3, 1, 2):
+        precondition(0, j)
     line_first(0)
     factors(0, held > 0)
     to_smem.wait()
     line_pool(0)
-    steps(0, 2)
+    steps(0, 1)
     line_second(0)
     x_rest(2)
     x_forward(3)
-    steps(2, 4)
+    steps(1, 2)
+    x_held(2)
     x_done(2)
     mix(1)
+    x_held(3)
+    precondition(1, 0)
+    steps(2, 4)
+    x_rest(3)
     steps(4, 6)
-    x_rest(3)
-    steps(6, 8)
     x_done(3)
-    precondition(1)
+    for j in (3, 1, 2):
+        precondition(1, j)
     line_first(1)
     scale_first()
-    steps(8, SECOND)
+    steps(6, SECOND)
     line_pool(1)
     steps(SECOND, SECOND + 3)
     line_second(1)
     scale_second()
     factors(1, held > 1)
+    put(2, left_new, left_o)
+    put(3, right_new, right_o)
     steps(SECOND + 3, SECOND + 8)
+    put_steps(0, SECOND + 5, 4)
     scale_third()
-    steps(SECOND + 8, STEPS + LAG + LAG_Y)
-
-    def put(i, src, dst):
-        return pltpu.make_async_copy(src, dst, outsem.at[i])
-
-    puts = [put(0, zland, zout), put(1, ynear, nout)]
-    for p in puts:
-        p.start()
+    steps(SECOND + 8, SECOND + 18)
+    put_steps(SECOND + 5, SECOND + 14, 5)
+    put(6, ynear.at[:, : SECOND + 9], nout.at[:, : SECOND + 9])
     for s in range(2):
         for i in (2, 3, 4):
             for k in (1, 3, 2):
                 line_recv(s, k, i).wait_recv()
-    more = [put(2, ol, lout)]
-    more[0].start()
+    put(7, ol, lout)
     for k in range(1, 8):
         sz_recv(k).wait_recv()
-    more.append(put(3, rz, sout))
-    more[1].start()
+    put(8, rz, sout)
+    steps(SECOND + 18, STEPS)
+    put_steps(SECOND + 14, STEPS - LAG, 9)
+    steps(STEPS, STEPS + LAG)
+    put_steps(STEPS - LAG, STEPS, 10)
+    steps(STEPS + LAG, STEPS + LAG + LAG_Y)
+    put(11, ynear.at[:, SECOND + 9 :], nout.at[:, SECOND + 9 :])
     for t in range(STEPS):
         for way in range(2):
             p_copy(way, t).wait_recv()
-    more.append(put(4, yopp, oout))
-    more[2].start()
+    put(12, yopp, oout)
     for w in range(4):
         x_drain(w)
     for s in range(2):
@@ -477,69 +537,90 @@
         sz_copy(k).wait_send()
     for k in range(1, 4):
         sy_copy(k).wait_send()
-    for p in puts + more:
+    for p in puts:
         p.wait()
 
 
-def spread_kernel(finds, zp, near, opp, line, scales, out, zv, nv, ov, lv, sv, flat, rows_out, insem, outsem):
+def spread_kernel(
+    finds, zp, near, opp, line, scales, left, right, second, out, left_new, right_new, second_new,
+    zv, nv, ov, lv, sv, rows_out, held, insem, outsem,
+):
     _, y, _, _ = me()
-    pairs = [(zp, zv), (near, nv), (opp, ov), (line, lv), (scales, sv)]
-    loads = [pltpu.make_async_copy(a, b, insem.at[i]) for i, (a, b) in enumerate(pairs)]
-    for k in loads:
+    pairs = [(scales, sv), (line, lv), (zp, zv), (near, nv), (opp, ov)]
+    pairs += [(left, held.at[0]), (right, held.at[1]), (second, held.at[2])]
+    moves = [pltpu.make_async_copy(a, b, insem.at[i]) for i, (a, b) in enumerate(pairs)]
+    for k in moves:
         k.start()
-    for k in loads:
+    for k in moves[:5]:
         k.wait()
-
-    def store(b, src):
-        keep = b % 4
-        scale = sv[finds[4, b], finds[5, b], pl.ds(finds[6, b], 1), :]
-
+    for i, ref in enumerate((left_new, right_new, second_new)):
+        moves[5 + i].wait()
+        moves[5 + i] = pltpu.make_async_copy(held.at[i], ref, insem.at[5 + i])
+        moves[5 + i].start()
+
+    def back(b):
+        return pltpu.make_async_copy(rows_out.at[b % 4], out.at[b], outsem.at[b % 4])
+
+    def store(b, pieces):
         @pl.when(b >= 4)
         def _():
-            pltpu.make_async_copy(rows_out.at[keep], out.at[b - 4], outsem.at[keep]).wait()
-
-        for col in range(8):
-            part = src(col).astype(F32) * scale
-            rows_out[keep, :, col * 128 : col * 128 + 128] = part.astype(BF)
-        pltpu.make_async_copy(rows_out.at[keep], out.at[b], outsem.at[keep]).start()
-
-    def one(b, _):
+            back(b - 4).wait()
+
+        scale = sv[finds[4, b], finds[5, b], pl.ds(finds[6, b], 1), :]
+        tile = 0
+        for count, get in pieces:
+            for i in range(count):
+                r, col = tile % 8 * 16, tile // 8 * 128
+                part = get(i * 16).astype(F32) * scale
+                rows_out[b % 4, r : r + 16, col : col + 128] = part.astype(BF)
+                tile += 1
+        back(b).start()
+
+    def one(b, yy):
         tp, tm = finds[0, b], finds[1, b]
 
         @pl.when(finds[2, b] == 1)
         def _():
             e = finds[3, b]
-            store(b, lambda col: lv[e, col * 128 : col * 128 + 128, :])
+            store(b, [(64, lambda lo: lv[e, lo : lo + 16, :])])
 
         @pl.when(finds[2, b] == 0)
         def _():
-            flat[:HALF_A] = zv[0, tp, :HALF_A]
-            flat[HALF_A : 2 * HALF_A] = zv[1, tm, :HALF_A]
-
-            def quarter(q, plus, minus):
-                lo = pl.multiple_of(FIRST_B + QUARTER * (q % NY), 16)
-                flat[pl.ds(lo, HALF_B)] = plus
-                flat[pl.ds(pl.multiple_of(lo + HALF_B, 16), HALF_B)] = minus
-
-            quarter(y, zv[0, tp, HALF_A:], zv[1, tm, HALF_A:])
-            quarter(y + NY - 1, nv[0, tp, :HALF_B], nv[0, tm, HALF_B:])
-            quarter(y + 1, nv[1, tp, :HALF_B], nv[1, tm, HALF_B:])
-            quarter(y + 2, ov[0, tp], ov[1, tm])
-            store(b, lambda col: flat[col * 128 : col * 128 + 128])
-
-        return 0
-
-    lax.fori_loop(0, 32, one, 0)
+            def tiles(ref, lead, lo, n):
+                return (n // 16, lambda at: ref[(*lead, slice(lo + at, lo + at + 16))])
+
+            quarters = {
+                yy: (tiles(zv, (0, tp), HALF_A, HALF_B), tiles(zv, (1, tm), HALF_A, HALF_B)),
+                (yy + 3) % NY: (tiles(nv, (0, tp), 0, HALF_B), tiles(nv, (0, tm), HALF_B, HALF_B)),
+                (yy + 1) % NY: (tiles(nv, (1, tp), 0, HALF_B), tiles(nv, (1, tm), HALF_B, HALF_B)),
+                (yy + 2) % NY: (tiles(ov, (0, tp), 0, HALF_B), tiles(ov, (1, tm), 0, HALF_B)),
+            }
+            pieces = [tiles(zv, (0, tp), 0, HALF_A), tiles(zv, (1, tm), 0, HALF_A)]
+            for q in range(NY):
+                pieces += quarters[q]
+            store(b, pieces)
+
+    for yy in range(NY):
+
+        @pl.when(y == yy)
+        def _(yy=yy):
+            def body(b, _):
+                one(b, yy)
+                return 0
+
+            lax.fori_loop(0, 32, body, 0)
+
     for b in range(28, 32):
-        pltpu.make_async_copy(rows_out.at[b % 4], out.at[b], outsem.at[b % 4]).wait()
+        back(b).wait()
+    for k in moves[5:]:
+        k.wait()
 
 
 def on_device(grads, left, right, left_root, right_root, second, owner):
-    owner_row = jnp.pad(owner, (0, 128 - owner.shape[0]), constant_values=-1).reshape(1, 128)
-    owner_col = jnp.broadcast_to(owner[:, None], (32, 128))
-    vmem, hbm = pl.BlockSpec(memory_space=pltpu.VMEM), pl.BlockSpec(memory_space=pl.ANY)
+    smem, hbm = pl.BlockSpec(memory_space=pltpu.SMEM), pl.BlockSpec(memory_space=pl.ANY)
     shape = jax.ShapeDtypeStruct
-    block = shape((SLOTS_DEV, ROWS, WIDTH), BF)
+    b_shape = (SLOTS_DEV, ROWS, WIDTH)
+    block = shape(b_shape, BF)
     z_shape, n_shape, o_shape = (2, STEPS, CHUNK, 128), (2, STEPS, QUARTER, 128), (2, STEPS, HALF_B, 128)
     l_shape, s_shape = (OWN, WIDTH, 128), (NZ, NY, 8, 128)
     dma = pltpu.SemaphoreType.DMA
@@ -549,11 +630,12 @@
             block, block, block, shape(z_shape, BF), shape(n_shape, BF), shape(o_shape, BF), shape(l_shape, BF),
             shape(s_shape, F32), shape((8, 128), I32),
         ),
-        in_specs=[vmem] * 8,
-        out_specs=(vmem, vmem, vmem, hbm, hbm, hbm, hbm, hbm, vmem),
-        scratch_shapes=[
+        in_specs=[hbm] * 6 + [smem],
+        out_specs=(hbm,) * 9,
+        scratch_shapes=[pltpu.VMEM(b_shape, BF)] * 8
+        + [
+            pltpu.VMEM((8, 128), I32),
             pltpu.VMEM((4, WIDTH, WIDTH), BF),
-            pltpu.VMEM((ROWS, WIDTH), BF),
             pltpu.VMEM((ROWS, WIDTH), BF),
             pltpu.VMEM((SLOTS_DEV, WIDTH, 128), BF),
             pltpu.VMEM(l_shape, BF),
@@ -570,34 +652,34 @@
             pltpu.VMEM((NY, 8, 128), F32),
             pltpu.VMEM(s_shape, F32),
             pltpu.VMEM((2, 8, 128), F32),
-            dma((4, 7)), dma((4, 7)),
+            dma((4, 10)), dma((4, 10)),
             dma((2, 3, 5)), dma((2, 3, 5)),
             dma((2, KEEP)), dma((2, STEPS)),
             dma((2, KEEP)), dma((2, STEPS)),
             dma((2, KEEP)), dma((2, STEPS)),
             dma((7,)), dma((7,)), dma((3,)), dma((3,)), dma((7,)), dma((7,)),
-            dma((1,)), dma((5,)),
+            dma((1,)), dma((9,)), dma((13,)),
         ],
         compiler_params=pltpu.CompilerParams(
-            collective_id=1, has_side_effects=True, vmem_limit_bytes=56 << 20
+            collective_id=1, has_side_effects=True, vmem_limit_bytes=60 << 20
         ),
         name="shampoo",
-    )(grads, left, right, left_root, right_root, second, owner_row, owner_col)
-    directions = pl.pallas_call(
+    )(grads, left, right, left_root, right_root, second, owner)
+    directions, left_new, right_new, second_new = pl.pallas_call(
         spread_kernel,
-        out_shape=shape((32, ROWS, WIDTH), BF),
-        in_specs=[pl.BlockSpec(memory_space=pltpu.SMEM)] + [hbm] * 5,
-        out_specs=hbm,
+        out_shape=(shape((32, ROWS, WIDTH), BF), block, block, block),
+        in_specs=[smem] + [hbm] * 8,
+        out_specs=(hbm,) * 4,
         scratch_shapes=[
             pltpu.VMEM(z_shape, BF), pltpu.VMEM(n_shape, BF), pltpu.VMEM(o_shape, BF), pltpu.VMEM(l_shape, BF),
             pltpu.VMEM(s_shape, F32),
-            pltpu.VMEM((WIDTH, 128), BF),
             pltpu.VMEM((4, ROWS, WIDTH), BF),
-            dma((5,)), dma((4,)),
+            pltpu.VMEM((3, *b_shape), BF),
+            dma((8,)), dma((4,)),
         ],
-        compiler_params=pltpu.CompilerParams(vmem_limit_bytes=48 << 20),
+        compiler_params=pltpu.CompilerParams(vmem_limit_bytes=60 << 20),
         name="spread",
-    )(finds, zp, near, opp, line, scales)
+    )(finds, zp, near, opp, line, scales, left_new, right_new, second_new)
     return (left_new, right_new, second_new, directions)
 
 

time: 160 us -> 137 us (0.86)
  Pallas kernels: 147 us -> 135 us
  local copies, waits for them, and re-layouts: 9.57 us -> 0 us
    pallas_call x1, Pallas kernels: 136 us -> 122 us  [on_device(): pl.pallas_call(main_kernel, out_shape=(block, block, block, shape(z_shape...]
    unnamed x17 -> x0, local copies, waits for them, and re-layouts: 7.07 us -> none
    pallas_call x1, Pallas kernels: 11.1 us -> 12.7 us  [on_device(): pl.pallas_call(spread_kernel, out_shape=(shape((32, ROWS, WIDTH), BF), bl...]
where the time goes in v2:
time: 137 us; the launch traced here: 136 us
  Pallas kernels  135 us (99%)
    pallas_call x1, Pallas kernels, on_device(): pl.pallas_call(main_kernel, out_shape=(block, block, block, shape(z_shape...  122 us
    pallas_call x1, Pallas kernels, on_device(): pl.pallas_call(spread_kernel, out_shape=(shape((32, ROWS, WIDTH), BF), bl...  12.7 us

profile of v2, /device:TPU:1, one launch (start us, length us, event | category | flops | bytes accessed | tf_op | source)
XLA Modules:
  0.0 135.7 jit_solution(10356530428913357415)
XLA Ops:
  0.6 122.3 %shampoo.1 = (bf16[2,128,1024]{2,1,0:T(8,128)(2,1)}, bf16[2,128,1024]{2,1,0:T(8,128)(2,1)}, bf16[2,128,1024]{2,1,0:T(8,128)(2,1)}, bf16[2,44,272,128]{3,2,1,0:T(...) custom-call(bf16[2,128,1024]{2,1,0:T(8,128)(2,1)} %grads_h.1, ...), custom_call_target="tpu_custom_call" | custom-call | tf_op jit(solution)/shard_map/shampoo/pallas_call | solution.py:627
  122.9 12.7 %spread.1 = (bf16[32,128,1024]{2,1,0:T(8,128)(2,1)}, bf16[2,128,1024]{2,1,0:T(8,128)(2,1)}, bf16[2,128,1024]{2,1,0:T(8,128)(2,1)}, bf16[2,128,1024]{2,1,0:T(8,128)(2,1)}) custom-call(s32[8,128]{1,0:T(8,128)} %get-tuple-element.17.finds, bf16[2,44,272,128]{3,2,1,0:T(8,128)(2,1)} %get-tuple-element.18.zp, bf16[2,44,160,128]{3,2,1,0:T(8,128)(2,1)} %get-tuple-element.19.near, ...), custom_call_target="tpu_custom_call" | custom-call | tf_op jit(solution)/shard_map/spread/pallas_call | solution.py:668

commit v3 on v2

--- a/solution.py
+++ b/solution.py
@@ -12,6 +12,7 @@
 
 NX, NY, NZ = 4, 4, 8
 ROWS, WIDTH, SLOTS_DEV = 128, 1024, 2
+PLACE = (0, 3, 1, 2)
 HALF_A = 192
 QUARTER = 160
 HALF_B = QUARTER // 2
@@ -22,6 +23,9 @@
 LAG_Y = 5
 SECOND = 10
 STEPS = 44
+DIRECT = STEPS - 6
+LAG_O = 3
+KEEP_Y = 16
 KEEP = 8
 ORDER = (
     (0, 0), (0, 1), (0, 2), (1, 0), (0, 3), (1, 1), (0, 4), (1, 2), (0, 5), (1, 3), (0, 6), (1, 4), (1, 5), (1, 6),
@@ -99,6 +103,7 @@
         line = jnp.sum((owner_col == (owner_row >> 2) * NY + k).astype(I32), axis=0, keepdims=True)
         line = jnp.broadcast_to(line, (8, 128))
         rank = rank + ((line > slot) & (yb > k)).astype(I32)
+    here = zb == z
     found = []
     for way, turn in enumerate((1, -1)):
         hops = (turn * (z - zb)) & 7
@@ -108,27 +113,22 @@
             for d in range(7):
                 st = jnp.sum(jnp.where(row == sender, start[way][p, d], 0), axis=0, keepdims=True)
                 came_at = jnp.where((hops == d + 1) & (slot == p), st + rank, came_at)
-        found.append(jnp.minimum(came_at, STEPS - 1))
-    here = (zb == z).astype(I32)
-    mine = slot * NY + yb
+        found.append(jnp.where(here, slot * NY + yb, OWN + came_at))
     finds = jnp.where(row == 0, found[0], 0)
     finds = jnp.where(row == 1, found[1], finds)
-    finds = jnp.where(row == 2, here, finds)
-    finds = jnp.where(row == 3, mine, finds)
-    finds = jnp.where(row == 4, zb, finds)
-    finds = jnp.where(row == 5, yb, finds)
-    finds = jnp.where(row == 6, slot, finds)
+    finds = jnp.where(row == 2, own, finds)
+    finds = jnp.where(row == 3, slot, finds)
     held = jnp.sum((own == z * NY + y).astype(I32), axis=1, keepdims=True)
     return tables, finds, held[:1]
 
 
 def main_kernel(
     grads_h, left_h, right_h, left_root_h, right_root_h, second_h, owner,
-    left_o, right_o, second_o, zout, nout, oout, lout, sout, finds_o,
-    grads, left, right, left_root, second, left_new, right_new, second_new, finds_out, xb, mixed, stack, ol, zland, pool, zst, yst, ynear, yopp,
+    left_o, right_o, second_o, blocks_o, sout, finds_o,
+    grads, left, right, left_root, second, left_new, right_new, second_new, finds_out, xb, mixed, stack, ol, zland, pool, zst, yst, ynear, yopp, rows_out,
     table_v, table_s, part, rk, ry, rz, tile,
     xsend, xrecv, osend, orecv, zsend, zrecv, nsend, nrecv, psend, precv,
-    rsend, rrecv, sysend, syrecv, szsend, szrecv, lsem, insem, outsem,
+    rsend, rrecv, sysend, syrecv, szsend, szrecv, lsem, insem, outsem, blocksem,
 ):
     z, y, x, c = me()
     rack = x * 2 + c
@@ -220,7 +220,7 @@
 
     def precondition(s, j):
         w = 2 * s + 1
-        at = ((x, after, two, prior)[j]) * 256
+        at = PLACE.index(j) * 256
         got = jnp.zeros((ROWS, 256), F32)
         for i in range(4):
             lhs = mixed[:, bcol((x + i) % NX)]
@@ -231,8 +231,8 @@
                 lhs, block, (((1,), (0 if here else 1,)), ((), ())), preferred_element_type=F32
             )
         got_b = got.astype(BF)
-        stack[s, pl.ds(pl.multiple_of(at, 256), 128), :] = got_b[:, :128]
-        stack[s, pl.ds(pl.multiple_of(at + 128, 128), 128), :] = got_b[:, 128:]
+        stack[s, at : at + 128, :] = got_b[:, :128]
+        stack[s, at + 128 : at + 256, :] = got_b[:, 128:]
         sq = got * got
         sq = jnp.sum((sq[:, :128] + sq[:, 128:]).reshape(16, 8, 128), axis=0)
         part[2 * s + 1] = sq if j == 0 else part[2 * s + 1] + sq
@@ -275,33 +275,29 @@
     def quarter(k):
         return pl.ds(pl.multiple_of(FIRST_B + QUARTER * k, 16), QUARTER)
 
+    def line_part(s, k, i, sender, receiver):
+        if i < 2:
+            rows = pl.ds(0, 256) if i == 0 else pl.ds(256, FIRST_B - 256)
+        else:
+            rows = quarter((receiver + i - 2) % NY)
+        return rcopy(
+            stack.at[s, rows], ol.at[s * NY + sender, rows], osend.at[s, k - 1, i], orecv.at[s, k - 1, i], ypeer[k]
+        )
+
     def line_copy(s, k, i):
-        to = (y + k) % NY
-        rows = pl.ds(0, FIRST_B) if i == 0 else quarter((to + i - 1) % NY)
-        return rcopy(
-            stack.at[s, rows], ol.at[s * NY + y, rows], osend.at[s, k - 1, i], orecv.at[s, k - 1, i], ypeer[k]
-        )
+        return line_part(s, k, i, y, (y + k) % NY)
 
     def line_recv(s, k, i):
-        frm = (y + NY - k) % NY
-        rows = pl.ds(0, FIRST_B) if i == 0 else quarter((y + i - 1) % NY)
-        return rcopy(
-            stack.at[s, rows], ol.at[s * NY + frm, rows], osend.at[s, k - 1, i], orecv.at[s, k - 1, i], ypeer[k]
-        )
-
-    def line_first(s):
-        for i in (0, 1):
+        return line_part(s, k, i, (y + NY - k) % NY, y)
+
+    def line_send(s, parts):
+        for i in parts:
             for k in (1, 3, 2):
                 line_copy(s, k, i).start()
+
+    def line_pool(s):
         ol[pl.ds(s * NY + y, 1)] = stack[s][None]
-
-    def line_second(s):
-        for i in (2, 3, 4):
-            for k in (1, 3, 2):
-                line_copy(s, k, i).start()
-
-    def line_pool(s):
-        for i in (0, 1):
+        for i in (0, 1, 2):
             for k in (1, 3, 2):
                 line_recv(s, k, i).wait_recv()
         for k in range(NY):
@@ -311,25 +307,44 @@
                 lo = pl.multiple_of(FIRST_B + QUARTER * y + way * HALF_B, 16)
                 pool[way, e, HALF_A:] = ol[e, pl.ds(lo, HALF_B), :]
 
+    def line_rest(s):
+        for i in (3, 4, 5):
+            for k in (1, 3, 2):
+                line_recv(s, k, i).wait_recv()
+        for k in range(NY):
+            e = s * NY + k
+            for way in range(2):
+                ynear[way, e] = ol[e, quarter((y + (3, 1)[way]) % NY), :]
+                lo = pl.multiple_of(FIRST_B + QUARTER * ((y + 2) % NY) + way * HALF_B, 16)
+                yopp[way, e] = ol[e, pl.ds(lo, HALF_B), :]
+
     def z_copy(way, t):
         return rcopy(
-            zst.at[way, t % KEEP], zland.at[way, t], zsend.at[way, t % KEEP], zrecv.at[way, t], zn[way]
+            zst.at[way, t % KEEP], zland.at[way, t], zsend.at[way, t % KEEP], zrecv.at[way, t % KEEP], zn[way]
         )
 
     def n_copy(way, t):
-        return rcopy(yst.at[t], ynear.at[way, t], nsend.at[way, t % KEEP], nrecv.at[way, t], yn[way])
-
-    def p_copy(way, t):
-        return rcopy(
-            ynear.at[way, t, pl.ds(way * HALF_B, HALF_B)], yopp.at[way, t],
-            psend.at[way, t % KEEP], precv.at[way, t], yn[way],
-        )
+        return rcopy(yst.at[t], ynear.at[way, OWN + t], nsend.at[way, t % KEEP], nrecv.at[way, t % KEEP_Y], yn[way])
+
+    def p_copy(way, t, direct=False):
+        half = pl.ds(way * HALF_B, HALF_B)
+        src = yst.at[t, half] if direct else ynear.at[way, OWN + t, half]
+        to = ypeer[2] if direct else yn[way]
+        recv = precv.at[way, KEEP_Y + t - DIRECT if direct else t % KEEP_Y]
+        return rcopy(src, yopp.at[way, OWN + t], psend.at[way, t % KEEP], recv, to)
+
+    def o_take(t):
+        for way in range(2):
+            p_copy(way, t).wait_recv()
+
+    def entry(*at):
+        return jnp.clip(table_s[at], 0, OWN + STEPS - 1)
 
     def z_send(t, again):
         for way in range(2):
             if again:
                 z_copy(way, t - KEEP).wait_send()
-            zst[way, t % KEEP] = pool[way, table_s[way, z, t]]
+            zst[way, t % KEEP] = pool[way, entry(way, z, t)]
             z_copy(way, t).start()
 
     def z_take(t):
@@ -345,17 +360,18 @@
                 n_copy(way, t - KEEP).wait_send()
             n_copy(way, t).start()
 
-    def y_take(t, again):
-        for way in range(2):
-            n_copy(way, t).wait_recv()
+    def y_take(t, again, direct):
+        for way in range(2):
+            if not direct:
+                n_copy(way, t).wait_recv()
             if again:
-                p_copy(way, t - KEEP).wait_send()
-            p_copy(way, t).start()
-
-    marks = sorted({0, LAG, LAG + LAG_Y, KEEP, KEEP + LAG, KEEP + LAG + LAG_Y, STEPS, STEPS + LAG, STEPS + LAG + LAG_Y})
+                p_copy(way, t - KEEP, direct).wait_send()
+            p_copy(way, t, direct).start()
+
+    marks = {0, LAG, LAG + LAG_Y, KEEP, KEEP + LAG, KEEP + LAG + LAG_Y, STEPS, STEPS + LAG, DIRECT + LAG, DIRECT + LAG + LAG_Y, LAG + LAG_Y + LAG_O}
 
     def steps(a, b):
-        cuts = [a] + [k for k in marks if a < k < b] + [b]
+        cuts = [a] + sorted(k for k in marks if a < k < b) + [b]
         for lo, hi in zip(cuts[:-1], cuts[1:]):
             def body(t, _, lo=lo):
                 if LAG <= lo < STEPS + LAG:
@@ -364,8 +380,12 @@
                     z_send(t, lo >= KEEP)
                 if LAG <= lo < STEPS + LAG:
                     y_send(t - LAG, lo - LAG >= KEEP)
-                if LAG + LAG_Y <= lo < STEPS + LAG + LAG_Y:
-                    y_take(t - LAG - LAG_Y, lo - LAG - LAG_Y >= KEEP)
+                if LAG + LAG_Y <= lo < DIRECT + LAG + LAG_Y:
+                    y_take(t - LAG - LAG_Y, lo - LAG - LAG_Y >= KEEP, False)
+                if DIRECT + LAG <= lo < STEPS + LAG:
+                    y_take(t - LAG, True, True)
+                if LAG + LAG_Y + LAG_O <= lo < STEPS + LAG:
+                    o_take(t - LAG - LAG_Y - LAG_O)
                 return 0
 
             lax.fori_loop(lo, hi, body, 0)
@@ -426,9 +446,6 @@
         copy.start()
         puts.append(copy)
 
-    def put_steps(lo, hi, i):
-        put(i, zland.at[:, lo:hi], zout.at[:, lo:hi])
-
     puts = []
     x_own(0)
     loads = [
@@ -443,6 +460,7 @@
     for way in range(2):
         table_v[way] = tables[way]
     finds_out[...] = finds
+    table_v[2] = finds
     to_smem = pltpu.make_async_copy(table_v, table_s, lsem.at[0])
     to_smem.start()
     x_forward(0)
@@ -461,18 +479,19 @@
     mix(0)
     x_held(1)
     precondition(0, 0)
+    line_send(0, (0,))
     x_rest(1)
     x_forward(2)
     x_own(3)
     x_done(1)
     for j in (3, 1, 2):
         precondition(0, j)
-    line_first(0)
+    line_send(0, (1, 2))
     factors(0, held > 0)
     to_smem.wait()
     line_pool(0)
     steps(0, 1)
-    line_second(0)
+    line_send(0, (3, 4, 5))
     x_rest(2)
     x_forward(3)
     steps(1, 2)
@@ -481,51 +500,69 @@
     mix(1)
     x_held(3)
     precondition(1, 0)
+    line_send(1, (0,))
     steps(2, 4)
     x_rest(3)
     steps(4, 6)
     x_done(3)
     for j in (3, 1, 2):
         precondition(1, j)
-    line_first(1)
+    line_send(1, (1, 2))
     scale_first()
     steps(6, SECOND)
     line_pool(1)
     steps(SECOND, SECOND + 3)
-    line_second(1)
+    line_send(1, (3, 4, 5))
     scale_second()
     factors(1, held > 1)
     put(2, left_new, left_o)
     put(3, right_new, right_o)
     steps(SECOND + 3, SECOND + 8)
-    put_steps(0, SECOND + 5, 4)
     scale_third()
     steps(SECOND + 8, SECOND + 18)
-    put_steps(SECOND + 5, SECOND + 14, 5)
-    put(6, ynear.at[:, : SECOND + 9], nout.at[:, : SECOND + 9])
     for s in range(2):
-        for i in (2, 3, 4):
-            for k in (1, 3, 2):
-                line_recv(s, k, i).wait_recv()
-    put(7, ol, lout)
+        line_rest(s)
     for k in range(1, 8):
         sz_recv(k).wait_recv()
-    put(8, rz, sout)
-    steps(SECOND + 18, STEPS)
-    put_steps(SECOND + 14, STEPS - LAG, 9)
-    steps(STEPS, STEPS + LAG)
-    put_steps(STEPS - LAG, STEPS, 10)
-    steps(STEPS + LAG, STEPS + LAG + LAG_Y)
-    put(11, ynear.at[:, SECOND + 9 :], nout.at[:, SECOND + 9 :])
-    for t in range(STEPS):
-        for way in range(2):
-            p_copy(way, t).wait_recv()
-    put(12, yopp, oout)
+    put(4, rz, sout)
+    steps(SECOND + 18, STEPS + LAG)
+    for t in range(DIRECT, STEPS):
+        for way in range(2):
+            n_copy(way, t).wait_recv()
+    for t in range(STEPS - LAG_Y - LAG_O, STEPS):
+        for way in range(2):
+            p_copy(way, t, t >= DIRECT).wait_recv()
+
+    def back(b):
+        return pltpu.make_async_copy(rows_out.at[b % 16], blocks_o.at[b], blocksem.at[b % 16])
+
+    def assemble(b, again):
+        plus, minus = entry(2, 0, b), entry(2, 1, b)
+        if again:
+            back(b - 16).wait()
+        keep = b % 16
+        rows_out[keep, :HALF_A] = pool[0, plus, :HALF_A]
+        rows_out[keep, HALF_A:FIRST_B] = pool[1, minus, :HALF_A]
+
+        def fill(q, first, last):
+            lo = pl.multiple_of(FIRST_B + QUARTER * (q % NY), 16)
+            rows_out[keep, pl.ds(lo, HALF_B)] = first
+            rows_out[keep, pl.ds(pl.multiple_of(lo + HALF_B, 16), HALF_B)] = last
+
+        fill(y, pool[0, plus, HALF_A:], pool[1, minus, HALF_A:])
+        fill(y + 3, ynear[0, plus, :HALF_B], ynear[0, minus, HALF_B:])
+        fill(y + 1, ynear[1, plus, :HALF_B], ynear[1, minus, HALF_B:])
+        fill(y + 2, yopp[0, plus], yopp[1, minus])
+        back(b).start()
+        return 0
+
+    lax.fori_loop(0, 16, lambda b, _: assemble(b, False), 0)
+    lax.fori_loop(16, 32, lambda b, _: assemble(b, True), 0)
     for w in range(4):
         x_drain(w)
     for s in range(2):
         for k in range(1, 4):
-            for i in range(5):
+            for i in range(6):
                 line_copy(s, k, i).wait_send()
     for t in range(STEPS - KEEP, STEPS):
         for way in range(2):
@@ -539,80 +576,61 @@
         sy_copy(k).wait_send()
     for p in puts:
         p.wait()
-
-
-def spread_kernel(
-    finds, zp, near, opp, line, scales, left, right, second, out, left_new, right_new, second_new,
-    zv, nv, ov, lv, sv, rows_out, held, insem, outsem,
+    for b in range(16, 32):
+        back(b).wait()
+
+
+def scale_kernel(
+    finds, blocks, scales, left, right, second, out, left_new, right_new, second_new,
+    flat, sv, rows_out, held, insem, blocksem, outsem,
 ):
-    _, y, _, _ = me()
-    pairs = [(scales, sv), (line, lv), (zp, zv), (near, nv), (opp, ov)]
-    pairs += [(left, held.at[0]), (right, held.at[1]), (second, held.at[2])]
-    moves = [pltpu.make_async_copy(a, b, insem.at[i]) for i, (a, b) in enumerate(pairs)]
-    for k in moves:
+    _, _, x, _ = me()
+    first = pltpu.make_async_copy(scales, sv, insem.at[3])
+    first.start()
+
+    def fetch(b):
+        return pltpu.make_async_copy(blocks.at[b], flat.at[b], blocksem.at[b])
+
+    def begin(b, _):
+        fetch(b).start()
+        return 0
+
+    lax.fori_loop(0, 8, begin, 0)
+    through = [
+        pltpu.make_async_copy(ref, held.at[i], insem.at[i]) for i, ref in enumerate((left, right, second))
+    ]
+    for k in through:
         k.start()
-    for k in moves[:5]:
-        k.wait()
+    lax.fori_loop(8, 32, begin, 0)
+    first.wait()
+
+    def back(b):
+        return pltpu.make_async_copy(rows_out.at[b % 8], out.at[b], outsem.at[b % 8])
+
+    def one(b, again):
+        owner = jnp.clip(finds[2, b], 0, NY * NZ - 1)
+        scale = sv[owner // NY, owner % NY, pl.ds(jnp.clip(finds[3, b], 0, 1), 1), :]
+        fetch(b).wait()
+        if again:
+            back(b - 8).wait()
+        for i, j in enumerate(PLACE):
+            for half in range(2):
+                row = (2 * i + half) * 128
+                col = pl.multiple_of((x + j) % NX * 256 + half * 128, 128)
+                part = flat[b, row : row + 128, :].astype(F32) * scale
+                rows_out[b % 8, :, pl.ds(col, 128)] = part.astype(BF)
+        back(b).start()
+        return 0
+
+    lax.fori_loop(0, 8, lambda b, _: one(b, False), 0)
     for i, ref in enumerate((left_new, right_new, second_new)):
-        moves[5 + i].wait()
-        moves[5 + i] = pltpu.make_async_copy(held.at[i], ref, insem.at[5 + i])
-        moves[5 + i].start()
-
-    def back(b):
-        return pltpu.make_async_copy(rows_out.at[b % 4], out.at[b], outsem.at[b % 4])
-
-    def store(b, pieces):
-        @pl.when(b >= 4)
-        def _():
-            back(b - 4).wait()
-
-        scale = sv[finds[4, b], finds[5, b], pl.ds(finds[6, b], 1), :]
-        tile = 0
-        for count, get in pieces:
-            for i in range(count):
-                r, col = tile % 8 * 16, tile // 8 * 128
-                part = get(i * 16).astype(F32) * scale
-                rows_out[b % 4, r : r + 16, col : col + 128] = part.astype(BF)
-                tile += 1
-        back(b).start()
-
-    def one(b, yy):
-        tp, tm = finds[0, b], finds[1, b]
-
-        @pl.when(finds[2, b] == 1)
-        def _():
-            e = finds[3, b]
-            store(b, [(64, lambda lo: lv[e, lo : lo + 16, :])])
-
-        @pl.when(finds[2, b] == 0)
-        def _():
-            def tiles(ref, lead, lo, n):
-                return (n // 16, lambda at: ref[(*lead, slice(lo + at, lo + at + 16))])
-
-            quarters = {
-                yy: (tiles(zv, (0, tp), HALF_A, HALF_B), tiles(zv, (1, tm), HALF_A, HALF_B)),
-                (yy + 3) % NY: (tiles(nv, (0, tp), 0, HALF_B), tiles(nv, (0, tm), HALF_B, HALF_B)),
-                (yy + 1) % NY: (tiles(nv, (1, tp), 0, HALF_B), tiles(nv, (1, tm), HALF_B, HALF_B)),
-                (yy + 2) % NY: (tiles(ov, (0, tp), 0, HALF_B), tiles(ov, (1, tm), 0, HALF_B)),
-            }
-            pieces = [tiles(zv, (0, tp), 0, HALF_A), tiles(zv, (1, tm), 0, HALF_A)]
-            for q in range(NY):
-                pieces += quarters[q]
-            store(b, pieces)
-
-    for yy in range(NY):
-
-        @pl.when(y == yy)
-        def _(yy=yy):
-            def body(b, _):
-                one(b, yy)
-                return 0
-
-            lax.fori_loop(0, 32, body, 0)
-
-    for b in range(28, 32):
+        through[i].wait()
+        through[i] = pltpu.make_async_copy(held.at[i], ref, insem.at[i])
+        through[i].start()
+    lax.fori_loop(8, 32, lambda b, _: one(b, True), 0)
+    for b in range(24, 32):
         back(b).wait()
-    for k in moves[5:]:
+    for k in through:
         k.wait()
 
 
@@ -621,44 +639,45 @@
     shape = jax.ShapeDtypeStruct
     b_shape = (SLOTS_DEV, ROWS, WIDTH)
     block = shape(b_shape, BF)
-    z_shape, n_shape, o_shape = (2, STEPS, CHUNK, 128), (2, STEPS, QUARTER, 128), (2, STEPS, HALF_B, 128)
-    l_shape, s_shape = (OWN, WIDTH, 128), (NZ, NY, 8, 128)
+    s_shape = (NZ, NY, 8, 128)
+    stacked = (32, WIDTH, 128)
+    entries = OWN + STEPS
     dma = pltpu.SemaphoreType.DMA
-    left_new, right_new, second_new, zp, near, opp, line, scales, finds = pl.pallas_call(
+    left_new, right_new, second_new, blocks, scales, finds = pl.pallas_call(
         main_kernel,
         out_shape=(
-            block, block, block, shape(z_shape, BF), shape(n_shape, BF), shape(o_shape, BF), shape(l_shape, BF),
-            shape(s_shape, F32), shape((8, 128), I32),
+            block, block, block, shape(stacked, BF), shape(s_shape, F32), shape((8, 128), I32),
         ),
         in_specs=[hbm] * 6 + [smem],
-        out_specs=(hbm,) * 9,
+        out_specs=(hbm,) * 6,
         scratch_shapes=[pltpu.VMEM(b_shape, BF)] * 8
         + [
             pltpu.VMEM((8, 128), I32),
             pltpu.VMEM((4, WIDTH, WIDTH), BF),
             pltpu.VMEM((ROWS, WIDTH), BF),
             pltpu.VMEM((SLOTS_DEV, WIDTH, 128), BF),
-            pltpu.VMEM(l_shape, BF),
-            pltpu.VMEM(z_shape, BF),
-            pltpu.VMEM((2, OWN + STEPS, CHUNK, 128), BF),
+            pltpu.VMEM((OWN, WIDTH, 128), BF),
+            pltpu.VMEM((2, STEPS, CHUNK, 128), BF),
+            pltpu.VMEM((2, entries, CHUNK, 128), BF),
             pltpu.VMEM((2, KEEP, CHUNK, 128), BF),
             pltpu.VMEM((STEPS, QUARTER, 128), BF),
-            pltpu.VMEM(n_shape, BF),
-            pltpu.VMEM(o_shape, BF),
-            pltpu.VMEM((2, 8, 128), I32),
-            pltpu.SMEM((2, 8, 128), I32),
+            pltpu.VMEM((2, entries, QUARTER, 128), BF),
+            pltpu.VMEM((2, entries, HALF_B, 128), BF),
+            pltpu.VMEM((16, WIDTH, 128), BF),
+            pltpu.VMEM((3, 8, 128), I32),
+            pltpu.SMEM((3, 8, 128), I32),
             pltpu.VMEM((4, 8, 128), F32),
             pltpu.VMEM((8, 8, 128), F32),
             pltpu.VMEM((NY, 8, 128), F32),
             pltpu.VMEM(s_shape, F32),
             pltpu.VMEM((2, 8, 128), F32),
             dma((4, 10)), dma((4, 10)),
-            dma((2, 3, 5)), dma((2, 3, 5)),
-            dma((2, KEEP)), dma((2, STEPS)),
-            dma((2, KEEP)), dma((2, STEPS)),
-            dma((2, KEEP)), dma((2, STEPS)),
+            dma((2, 3, 6)), dma((2, 3, 6)),
+            dma((2, KEEP)), dma((2, KEEP)),
+            dma((2, KEEP)), dma((2, KEEP_Y)),
+            dma((2, KEEP)), dma((2, KEEP_Y + STEPS - DIRECT)),
             dma((7,)), dma((7,)), dma((3,)), dma((3,)), dma((7,)), dma((7,)),
-            dma((1,)), dma((9,)), dma((13,)),
+            dma((1,)), dma((9,)), dma((5,)), dma((16,)),
         ],
         compiler_params=pltpu.CompilerParams(
             collective_id=1, has_side_effects=True, vmem_limit_bytes=60 << 20
@@ -666,20 +685,20 @@
         name="shampoo",
     )(grads, left, right, left_root, right_root, second, owner)
     directions, left_new, right_new, second_new = pl.pallas_call(
-        spread_kernel,
+        scale_kernel,
         out_shape=(shape((32, ROWS, WIDTH), BF), block, block, block),
-        in_specs=[smem] + [hbm] * 8,
+        in_specs=[smem] + [hbm] * 5,
         out_specs=(hbm,) * 4,
         scratch_shapes=[
-            pltpu.VMEM(z_shape, BF), pltpu.VMEM(n_shape, BF), pltpu.VMEM(o_shape, BF), pltpu.VMEM(l_shape, BF),
+            pltpu.VMEM(stacked, BF),
             pltpu.VMEM(s_shape, F32),
-            pltpu.VMEM((4, ROWS, WIDTH), BF),
+            pltpu.VMEM((8, ROWS, WIDTH), BF),
             pltpu.VMEM((3, *b_shape), BF),
-            dma((8,)), dma((4,)),
+            dma((4,)), dma((32,)), dma((8,)),
         ],
         compiler_params=pltpu.CompilerParams(vmem_limit_bytes=60 << 20),
         name="spread",
-    )(finds, zp, near, opp, line, scales, left_new, right_new, second_new)
+    )(finds, blocks, scales, left_new, right_new, second_new)
     return (left_new, right_new, second_new, directions)
 
 

time: 137 us -> 134 us (0.978)
  Pallas kernels: 135 us -> 133 us
    pallas_call x2, Pallas kernels: 135 us -> 133 us  [the longest x1 124 us: on_device(): pl.pallas_call(main_kernel, out_shape=(block, block, block, shape(stacked...]
where the time goes in v3:
time: 134 us
  Pallas kernels  133 us (99%)
    pallas_call x1, Pallas kernels, on_device(): pl.pallas_call(main_kernel, out_shape=(block, block, block, shape(stacked...  124 us
    pallas_call x1, Pallas kernels, on_device(): pl.pallas_call(scale_kernel, out_shape=(shape((32, ROWS, WIDTH), BF), blo...  8.71 us

profile of v3, /device:TPU:1, one launch (start us, length us, event | category | flops | bytes accessed | tf_op | source)
XLA Modules:
  0.0 133.6 jit_solution(15819752573584783648)
XLA Ops:
  0.6 124.3 %shampoo.1 = (bf16[2,128,1024]{2,1,0:T(8,128)(2,1)}, bf16[2,128,1024]{2,1,0:T(8,128)(2,1)}, bf16[2,128,1024]{2,1,0:T(8,128)(2,1)}, bf16[32,1024,128]{2,1,0:T(8,1...) custom-call(bf16[2,128,1024]{2,1,0:T(8,128)(2,1)} %grads_h.1, bf16[2,128,1024]{2,1,0:T(8,128)(2,1)} %left_h.1, ...), custom_call_target="tpu_custom_call" | custom-call | tf_op jit(solution)/shard_map/shampoo/pallas_call | solution.py:646
  124.9 8.7 %spread.1 = (bf16[32,128,1024]{2,1,0:T(8,128)(2,1)}, bf16[2,128,1024]{2,1,0:T(8,128)(2,1)}, bf16[2,128,1024]{2,1,0:T(8,128)(2,1)}, bf16[2,128,1024]{2,1,0:T(8,128)(2,1)}) custom-call(s32[8,128]{1,0:T(8,128)} %get-tuple-element.14.finds, bf16[32,1024,128]{2,1,0:T(8,128)(2,1)} %get-tuple-element.15.blocks, f32[8,4,8,128]{3,2,1,0:T(8,128)} %get-tuple-element.16.scales, ...), custom_call_target="tpu_custom_call" | custom-call | tf_op jit(solution)/shard_map/spread/pallas_call | solution.py:687

commit v4 on v3

--- a/solution.py
+++ b/solution.py
@@ -20,10 +20,10 @@
 CHUNK = HALF_A + HALF_B
 OWN = SLOTS_DEV * NY
 LAG = 3
-LAG_Y = 5
+LAG_Y = 3
 SECOND = 10
-STEPS = 44
-DIRECT = STEPS - 6
+VARIANTS = (36, 38, 44)
+LAST = 4
 LAG_O = 3
 KEEP_Y = 16
 KEEP = 8
@@ -68,6 +68,7 @@
     before = [[sum(u[:k], jnp.zeros((8, 128), I32)) for k in range(NY)] for u in used]
     start = []
     tables = []
+    ends = []
     for turn in (1, -1):
         st = {}
         end = jnp.zeros((8, 128), I32)
@@ -92,6 +93,7 @@
                 entry = OWN + came + spot
             table = jnp.where((lane >= at) & (lane < end), entry, table)
         start.append(st)
+        ends.append(end)
         tables.append(table)
     earlier = (owner_col == owner_row) & (
         lax.broadcasted_iota(I32, (32, 128), 0) < lax.broadcasted_iota(I32, (32, 128), 1)
@@ -119,17 +121,33 @@
     finds = jnp.where(row == 2, own, finds)
     finds = jnp.where(row == 3, slot, finds)
     held = jnp.sum((own == z * NY + y).astype(I32), axis=1, keepdims=True)
-    return tables, finds, held[:1]
+    finds = jnp.where(row == 4, held, finds)
+    ends = jnp.maximum(ends[0], ends[1])
+    return tables, finds, jnp.max(ends)
+
+
+def plan_kernel(owner, tables_o, finds_o, which_o):
+    z, y, _, _ = me()
+    tables, finds, ends = schedule(owner, z, y)
+    for way in range(2):
+        tables_o[way] = tables[way]
+    tables_o[2] = finds
+    finds_o[...] = finds
+    which = jnp.int32(0)
+    for some in VARIANTS[:-1]:
+        which = which + (ends > some).astype(I32)
+    which_o[0] = which
 
 
 def main_kernel(
-    grads_h, left_h, right_h, left_root_h, right_root_h, second_h, owner,
-    left_o, right_o, second_o, blocks_o, sout, finds_o,
-    grads, left, right, left_root, second, left_new, right_new, second_new, finds_out, xb, mixed, stack, ol, zland, pool, zst, yst, ynear, yopp, rows_out,
-    table_v, table_s, part, rk, ry, rz, tile,
+    STEPS, grads_h, left_h, right_h, left_root_h, right_root_h, second_h, tables_h,
+    left_o, right_o, second_o, blocks_o, sout,
+    grads, left, right, left_root, second, left_new, right_new, second_new, xb, mixed, stack, ol, zland, pool, zst, yst, ynear, yopp, rows_out,
+    table_s, part, rk, ry, rz, tile,
     xsend, xrecv, osend, orecv, zsend, zrecv, nsend, nrecv, psend, precv,
     rsend, rrecv, sysend, syrecv, szsend, szrecv, lsem, insem, outsem, blocksem,
 ):
+    DIRECT = STEPS - LAST
     z, y, x, c = me()
     rack = x * 2 + c
     xp, xm = dev(z, y, (x + 1) % NX, c), dev(z, y, (x + NX - 1) % NX, c)
@@ -456,21 +474,17 @@
     ]
     for k in loads:
         k.start()
-    tables, finds, held = schedule(owner, z, y)
-    for way in range(2):
-        table_v[way] = tables[way]
-    finds_out[...] = finds
-    table_v[2] = finds
-    to_smem = pltpu.make_async_copy(table_v, table_s, lsem.at[0])
+    to_smem = pltpu.make_async_copy(tables_h, table_s, lsem.at[0])
     to_smem.start()
     x_forward(0)
     x_own(1)
     for k in loads:
         k.wait()
-    put(0, finds_out, finds_o)
+    to_smem.wait()
+    held = jnp.zeros((1, 1), I32) + table_s[2, 4, 0]
     graft(0, held > 0)
     graft(1, held > 1)
-    put(1, second_new, second_o)
+    put(0, second_new, second_o)
     x_rest(0)
     x_forward(1)
     x_own(2)
@@ -488,10 +502,8 @@
         precondition(0, j)
     line_send(0, (1, 2))
     factors(0, held > 0)
-    to_smem.wait()
     line_pool(0)
     steps(0, 1)
-    line_send(0, (3, 4, 5))
     x_rest(2)
     x_forward(3)
     steps(1, 2)
@@ -512,20 +524,30 @@
     steps(6, SECOND)
     line_pool(1)
     steps(SECOND, SECOND + 3)
-    line_send(1, (3, 4, 5))
     scale_second()
     factors(1, held > 1)
     put(2, left_new, left_o)
     put(3, right_new, right_o)
-    steps(SECOND + 3, SECOND + 8)
+    steps(SECOND + 3, SECOND + 5)
+    line_send(0, (3,))
+    steps(SECOND + 5, SECOND + 8)
+    line_send(0, (4,))
     scale_third()
-    steps(SECOND + 8, SECOND + 18)
+    steps(SECOND + 8, SECOND + 10)
+    line_send(0, (5,))
+    steps(SECOND + 10, SECOND + 12)
+    line_send(1, (3,))
+    steps(SECOND + 12, SECOND + 15)
+    line_send(1, (4,))
+    steps(SECOND + 15, SECOND + 18)
+    line_send(1, (5,))
+    steps(SECOND + 18, SECOND + 26)
     for s in range(2):
         line_rest(s)
     for k in range(1, 8):
         sz_recv(k).wait_recv()
-    put(4, rz, sout)
-    steps(SECOND + 18, STEPS + LAG)
+    put(1, rz, sout)
+    steps(SECOND + 26, STEPS + LAG)
     for t in range(DIRECT, STEPS):
         for way in range(2):
             n_copy(way, t).wait_recv()
@@ -636,54 +658,69 @@
 
 def on_device(grads, left, right, left_root, right_root, second, owner):
     smem, hbm = pl.BlockSpec(memory_space=pltpu.SMEM), pl.BlockSpec(memory_space=pl.ANY)
+    vmem = pl.BlockSpec(memory_space=pltpu.VMEM)
     shape = jax.ShapeDtypeStruct
     b_shape = (SLOTS_DEV, ROWS, WIDTH)
     block = shape(b_shape, BF)
+    tables, finds, which = pl.pallas_call(
+        plan_kernel,
+        out_shape=(shape((3, 8, 128), I32), shape((8, 128), I32), shape((1,), I32)),
+        in_specs=[smem],
+        out_specs=(vmem, vmem, smem),
+        name="plan",
+    )(owner)
     s_shape = (NZ, NY, 8, 128)
+    dma = pltpu.SemaphoreType.DMA
     stacked = (32, WIDTH, 128)
-    entries = OWN + STEPS
-    dma = pltpu.SemaphoreType.DMA
-    left_new, right_new, second_new, blocks, scales, finds = pl.pallas_call(
-        main_kernel,
-        out_shape=(
-            block, block, block, shape(stacked, BF), shape(s_shape, F32), shape((8, 128), I32),
-        ),
-        in_specs=[hbm] * 6 + [smem],
-        out_specs=(hbm,) * 6,
-        scratch_shapes=[pltpu.VMEM(b_shape, BF)] * 8
-        + [
-            pltpu.VMEM((8, 128), I32),
-            pltpu.VMEM((4, WIDTH, WIDTH), BF),
-            pltpu.VMEM((ROWS, WIDTH), BF),
-            pltpu.VMEM((SLOTS_DEV, WIDTH, 128), BF),
-            pltpu.VMEM((OWN, WIDTH, 128), BF),
-            pltpu.VMEM((2, STEPS, CHUNK, 128), BF),
-            pltpu.VMEM((2, entries, CHUNK, 128), BF),
-            pltpu.VMEM((2, KEEP, CHUNK, 128), BF),
-            pltpu.VMEM((STEPS, QUARTER, 128), BF),
-            pltpu.VMEM((2, entries, QUARTER, 128), BF),
-            pltpu.VMEM((2, entries, HALF_B, 128), BF),
-            pltpu.VMEM((16, WIDTH, 128), BF),
-            pltpu.VMEM((3, 8, 128), I32),
-            pltpu.SMEM((3, 8, 128), I32),
-            pltpu.VMEM((4, 8, 128), F32),
-            pltpu.VMEM((8, 8, 128), F32),
-            pltpu.VMEM((NY, 8, 128), F32),
-            pltpu.VMEM(s_shape, F32),
-            pltpu.VMEM((2, 8, 128), F32),
-            dma((4, 10)), dma((4, 10)),
-            dma((2, 3, 6)), dma((2, 3, 6)),
-            dma((2, KEEP)), dma((2, KEEP)),
-            dma((2, KEEP)), dma((2, KEEP_Y)),
-            dma((2, KEEP)), dma((2, KEEP_Y + STEPS - DIRECT)),
-            dma((7,)), dma((7,)), dma((3,)), dma((3,)), dma((7,)), dma((7,)),
-            dma((1,)), dma((9,)), dma((5,)), dma((16,)),
-        ],
-        compiler_params=pltpu.CompilerParams(
-            collective_id=1, has_side_effects=True, vmem_limit_bytes=60 << 20
-        ),
-        name="shampoo",
-    )(grads, left, right, left_root, right_root, second, owner)
+
+    def run(i, *args):
+        STEPS = VARIANTS[i]
+        entries = OWN + STEPS
+        return pl.pallas_call(
+            functools.partial(main_kernel, STEPS),
+            out_shape=(
+                block, block, block, shape(stacked, BF), shape(s_shape, F32),
+            ),
+            in_specs=[hbm] * 7,
+            out_specs=(hbm,) * 5,
+            scratch_shapes=[pltpu.VMEM(b_shape, BF)] * 8
+            + [
+                pltpu.VMEM((4, WIDTH, WIDTH), BF),
+                pltpu.VMEM((ROWS, WIDTH), BF),
+                pltpu.VMEM((SLOTS_DEV, WIDTH, 128), BF),
+                pltpu.VMEM((OWN, WIDTH, 128), BF),
+                pltpu.VMEM((2, STEPS, CHUNK, 128), BF),
+                pltpu.VMEM((2, entries, CHUNK, 128), BF),
+                pltpu.VMEM((2, KEEP, CHUNK, 128), BF),
+                pltpu.VMEM((STEPS, QUARTER, 128), BF),
+                pltpu.VMEM((2, entries, QUARTER, 128), BF),
+                pltpu.VMEM((2, entries, HALF_B, 128), BF),
+                pltpu.VMEM((16, WIDTH, 128), BF),
+                pltpu.SMEM((3, 8, 128), I32),
+                pltpu.VMEM((4, 8, 128), F32),
+                pltpu.VMEM((8, 8, 128), F32),
+                pltpu.VMEM((NY, 8, 128), F32),
+                pltpu.VMEM(s_shape, F32),
+                pltpu.VMEM((2, 8, 128), F32),
+                dma((4, 10)), dma((4, 10)),
+                dma((2, 3, 6)), dma((2, 3, 6)),
+                dma((2, KEEP)), dma((2, KEEP)),
+                dma((2, KEEP)), dma((2, KEEP_Y)),
+                dma((2, KEEP)), dma((2, KEEP_Y + LAST)),
+                dma((7,)), dma((7,)), dma((3,)), dma((3,)), dma((7,)), dma((7,)),
+                dma((1,)), dma((9,)), dma((4,)), dma((16,)),
+            ],
+            compiler_params=pltpu.CompilerParams(
+                collective_id=1 + i, has_side_effects=True, vmem_limit_bytes=60 << 20
+            ),
+            name="shampoo",
+        )(*args)
+
+    left_new, right_new, second_new, blocks, scales = lax.switch(
+        which[0],
+        [functools.partial(run, i) for i in range(len(VARIANTS))],
+        grads, left, right, left_root, right_root, second, tables,
+    )
     directions, left_new, right_new, second_new = pl.pallas_call(
         scale_kernel,
         out_shape=(shape((32, ROWS, WIDTH), BF), block, block, block),

time: 134 us -> 124 us (0.925)
  Pallas kernels: 133 us -> 123 us
    pallas_call x1 -> x2, Pallas kernels: 124 us -> 114 us  [the longest x1 113 us: run(): pl.pallas_call(functools.partial(main_kernel, STEPS), out_shape=(block, b...]
where the time goes in v4:
time: 124 us
  Pallas kernels  123 us (99%)
  between operations  1.5 us (1%)
    pallas_call x1, Pallas kernels, run(): pl.pallas_call(functools.partial(main_kernel, STEPS), out_shape=(block, b...  113 us
    pallas_call x1, Pallas kernels, on_device(): pl.pallas_call(scale_kernel, out_shape=(shape((32, ROWS, WIDTH), BF), blo...  8.22 us

profile of v4, /device:TPU:1, one launch (start us, length us, event | category | flops | bytes accessed | tf_op | source)
XLA Modules:
  0.0 124.3 jit_solution(16737429228260820024)
XLA Ops:
  0.6 1.6 %plan.1 = (s32[3,8,128]{2,1,0:T(8,128)S(1)}, s32[8,128]{1,0:T(8,128)}, s32[1]{0:T(128)}) custom-call(s32[32]{0:T(128)} %owner.1), custom_call_target="tpu_custom_call" | custom-call | tf_op jit(solution)/shard_map/plan/pallas_call | solution.py:665
  2.9 113.0 %conditional.1 = ((bf16[2,128,1024]{2,1,0:T(8,128)(2,1)S(1)}, bf16[2,128,1024]{2,1,0:T(8,128)(2,1)S(1)}, bf16[2,128,1024]{2,1,0:T(8,128)(2,1)S(1)}, bf16[32,1024,128]{2,1,0:T(8,128)(2,1)}, f32[8,4,8,128]{3,2,1,0:T(8,128)S(1)})) conditional(s32[]{:T(128)} %bitcast, (bf16[2,128,1024]{2,1,0:T(8,128)(2,1)}, ...), branch_computations={%region_0.0_spmd, %region_1.0_spmd, %region_2.0_spmd} | conditional | bytes 8 | solution.py:719
  2.9 112.7 %shampoo.3 = (bf16[2,128,1024]{2,1,0:T(8,128)(2,1)S(1)}, bf16[2,128,1024]{2,1,0:T(8,128)(2,1)S(1)}, bf16[2,128,1024]{2,1,0:T(8,128)(2,1)S(1)}, bf16[32,1024,128]{2,1,0:T(8,128)(2,1)}, f32[8,4,8,128]{3,2,1,0:T(8,128)S(1)}) custom-call(bf16[2,128,1024]{2,1,0:T(8,128)(2,1)} %get-tuple-element.42.grads_h, bf16[2,128,1024]{2,1,0:T(8,128)(2,1)} %get-tuple-element.43.left_h, ...), custom_call_target="tpu_custom_call" | custom-call | tf_op jit(solution)/shard_map/cond/branch_0_fun/shampoo/pallas_call | solution.py:679
  115.9 8.2 %spread.1 = (bf16[32,128,1024]{2,1,0:T(8,128)(2,1)}, bf16[2,128,1024]{2,1,0:T(8,128)(2,1)}, bf16[2,128,1024]{2,1,0:T(8,128)(2,1)}, bf16[2,128,1024]{2,1,0:T(8,128)(2,1)}) custom-call(s32[8,128]{1,0:T(8,128)} %get-tuple-element.79.finds, bf16[32,1024,128]{2,1,0:T(8,128)(2,1)} %get-tuple-element.82.blocks, f32[8,4,8,128]{3,2,1,0:T(8,128)S(1)} %get-tuple-element.83.scales, ...), custom_call_target="tpu_custom_call" | custom-call | tf_op jit(solution)/shard_map/spread/pallas_call | solution.py:724

commit v5 on v4

--- a/solution.py
+++ b/solution.py
@@ -144,7 +144,7 @@
     left_o, right_o, second_o, blocks_o, sout,
     grads, left, right, left_root, second, left_new, right_new, second_new, xb, mixed, stack, ol, zland, pool, zst, yst, ynear, yopp, rows_out,
     table_s, part, rk, ry, rz, tile,
-    xsend, xrecv, osend, orecv, zsend, zrecv, nsend, nrecv, psend, precv,
+    xsend, xrecv, osend, orecv, fsend, frecv, zsend, zrecv, nsend, nrecv, psend, precv,
     rsend, rrecv, sysend, syrecv, szsend, szrecv, lsem, insem, outsem, blocksem,
 ):
     DIRECT = STEPS - LAST
@@ -308,10 +308,30 @@
     def line_recv(s, k, i):
         return line_part(s, k, i, (y + NY - k) % NY, y)
 
+    def line_peers(i):
+        return (1, 3, 2) if i < 3 else (1, 3)
+
     def line_send(s, parts):
         for i in parts:
-            for k in (1, 3, 2):
+            for k in line_peers(i):
                 line_copy(s, k, i).start()
+
+    def onward(s, way, i, to):
+        e = s * NY + (to + 2) % NY
+        lo = FIRST_B + QUARTER * ((to + i) % NY) + way * HALF_B
+        rows = pl.ds(pl.multiple_of(lo, 16), HALF_B)
+        return rcopy(ol.at[e, rows], ol.at[e, rows], fsend.at[s, way, i - 1], frecv.at[s, way, i - 1], yn[way])
+
+    def onward_send(s, way, i):
+        return onward(s, way, i, (y + (1, 3)[way]) % NY)
+
+    def line_onward(s):
+        for i in (3, 4, 5):
+            for k in (1, 3):
+                line_recv(s, k, i).wait_recv()
+        for i in (1, 2, 3):
+            for way in range(2):
+                onward_send(s, way, i).start()
 
     def line_pool(s):
         ol[pl.ds(s * NY + y, 1)] = stack[s][None]
@@ -326,9 +346,9 @@
                 pool[way, e, HALF_A:] = ol[e, pl.ds(lo, HALF_B), :]
 
     def line_rest(s):
-        for i in (3, 4, 5):
-            for k in (1, 3, 2):
-                line_recv(s, k, i).wait_recv()
+        for i in (1, 2, 3):
+            for way in range(2):
+                onward(s, way, i, y).wait_recv()
         for k in range(NY):
             e = s * NY + k
             for way in range(2):
@@ -495,12 +515,12 @@
     precondition(0, 0)
     line_send(0, (0,))
     x_rest(1)
-    x_forward(2)
-    x_own(3)
     x_done(1)
     for j in (3, 1, 2):
         precondition(0, j)
     line_send(0, (1, 2))
+    x_forward(2)
+    x_own(3)
     factors(0, held > 0)
     line_pool(0)
     steps(0, 1)
@@ -528,20 +548,23 @@
     factors(1, held > 1)
     put(2, left_new, left_o)
     put(3, right_new, right_o)
-    steps(SECOND + 3, SECOND + 5)
+    steps(SECOND + 3, SECOND + 4)
     line_send(0, (3,))
-    steps(SECOND + 5, SECOND + 8)
+    steps(SECOND + 4, SECOND + 6)
     line_send(0, (4,))
     scale_third()
+    steps(SECOND + 6, SECOND + 8)
+    line_send(0, (5,))
     steps(SECOND + 8, SECOND + 10)
-    line_send(0, (5,))
+    line_send(1, (3,))
     steps(SECOND + 10, SECOND + 12)
-    line_send(1, (3,))
-    steps(SECOND + 12, SECOND + 15)
     line_send(1, (4,))
-    steps(SECOND + 15, SECOND + 18)
+    steps(SECOND + 12, SECOND + 14)
+    line_onward(0)
     line_send(1, (5,))
-    steps(SECOND + 18, SECOND + 26)
+    steps(SECOND + 14, SECOND + 20)
+    line_onward(1)
+    steps(SECOND + 20, SECOND + 26)
     for s in range(2):
         line_rest(s)
     for k in range(1, 8):
@@ -583,9 +606,12 @@
     for w in range(4):
         x_drain(w)
     for s in range(2):
-        for k in range(1, 4):
-            for i in range(6):
+        for i in range(6):
+            for k in line_peers(i):
                 line_copy(s, k, i).wait_send()
+        for i in (1, 2, 3):
+            for way in range(2):
+                onward_send(s, way, i).wait_send()
     for t in range(STEPS - KEEP, STEPS):
         for way in range(2):
             z_copy(way, t).wait_send()
@@ -703,7 +729,7 @@
                 pltpu.VMEM(s_shape, F32),
                 pltpu.VMEM((2, 8, 128), F32),
                 dma((4, 10)), dma((4, 10)),
-                dma((2, 3, 6)), dma((2, 3, 6)),
+                dma((2, 3, 6)), dma((2, 3, 6)), dma((2, 2, 3)), dma((2, 2, 3)),
                 dma((2, KEEP)), dma((2, KEEP)),
                 dma((2, KEEP)), dma((2, KEEP_Y)),
                 dma((2, KEEP)), dma((2, KEEP_Y + LAST)),

time: 124 us -> 120 us (0.968)
  Pallas kernels: 123 us -> 119 us
    pallas_call x1, Pallas kernels: 113 us -> 109 us  [run(): pl.pallas_call(functools.partial(main_kernel, STEPS), out_shape=(block, b...]
where the time goes in v5:
time: 120 us
  Pallas kernels  119 us (99%)
  between operations  1.5 us (1%)
    pallas_call x1, Pallas kernels, run(): pl.pallas_call(functools.partial(main_kernel, STEPS), out_shape=(block, b...  109 us
    pallas_call x1, Pallas kernels, on_device(): pl.pallas_call(scale_kernel, out_shape=(shape((32, ROWS, WIDTH), BF), blo...  8.22 us

profile of v5, /device:TPU:1, one launch (start us, length us, event | category | flops | bytes accessed | tf_op | source)
XLA Modules:
  0.0 120.3 jit_solution(3956272823805726628)
XLA Ops:
  0.6 1.6 %plan.1 = (s32[3,8,128]{2,1,0:T(8,128)S(1)}, s32[8,128]{1,0:T(8,128)}, s32[1]{0:T(128)}) custom-call(s32[32]{0:T(128)} %owner.1), custom_call_target="tpu_custom_call" | custom-call | tf_op jit(solution)/shard_map/plan/pallas_call | solution.py:691
  2.9 109.0 %conditional.1 = ((bf16[2,128,1024]{2,1,0:T(8,128)(2,1)S(1)}, bf16[2,128,1024]{2,1,0:T(8,128)(2,1)S(1)}, bf16[2,128,1024]{2,1,0:T(8,128)(2,1)S(1)}, bf16[32,1024,128]{2,1,0:T(8,128)(2,1)}, f32[8,4,8,128]{3,2,1,0:T(8,128)S(1)})) conditional(s32[]{:T(128)} %bitcast, (bf16[2,128,1024]{2,1,0:T(8,128)(2,1)}, ...), branch_computations={%region_0.0_spmd, %region_1.0_spmd, %region_2.0_spmd} | conditional | bytes 8 | solution.py:745
  2.9 108.7 %shampoo.3 = (bf16[2,128,1024]{2,1,0:T(8,128)(2,1)S(1)}, bf16[2,128,1024]{2,1,0:T(8,128)(2,1)S(1)}, bf16[2,128,1024]{2,1,0:T(8,128)(2,1)S(1)}, bf16[32,1024,128]{2,1,0:T(8,128)(2,1)}, f32[8,4,8,128]{3,2,1,0:T(8,128)S(1)}) custom-call(bf16[2,128,1024]{2,1,0:T(8,128)(2,1)} %get-tuple-element.42.grads_h, bf16[2,128,1024]{2,1,0:T(8,128)(2,1)} %get-tuple-element.43.left_h, ...), custom_call_target="tpu_custom_call" | custom-call | tf_op jit(solution)/shard_map/cond/branch_0_fun/shampoo/pallas_call | solution.py:705
  111.9 8.2 %spread.1 = (bf16[32,128,1024]{2,1,0:T(8,128)(2,1)}, bf16[2,128,1024]{2,1,0:T(8,128)(2,1)}, bf16[2,128,1024]{2,1,0:T(8,128)(2,1)}, bf16[2,128,1024]{2,1,0:T(8,128)(2,1)}) custom-call(s32[8,128]{1,0:T(8,128)} %get-tuple-element.79.finds, bf16[32,1024,128]{2,1,0:T(8,128)(2,1)} %get-tuple-element.82.blocks, f32[8,4,8,128]{3,2,1,0:T(8,128)S(1)} %get-tuple-element.83.scales, ...), custom_call_target="tpu_custom_call" | custom-call | tf_op jit(solution)/shard_map/spread/pallas_call | solution.py:750
